TPU v7x, 256 devices: a whole 4x4x8 slice. The times are simulated.
256 devices in a mesh: pairs: 32 (over x, y, core), tm: 8 (over z).
Axes of the slice: x: 4, y: 4, z: 8, core: 2. Of those that a mesh axis runs over, the one named last changes fastest.
Arguments:
- spectra: bfloat16 [2, 8, 1024, 4096], P(None, 'tm', 'pairs')
- pair_blocks: int32 [32, 4, 2], replicated, may hold values from 0 to 31, as said below
- block_count: int32 [32], replicated, may hold values from 1 to 4, as said below
Outputs:
- stacked: float32 [128, 128, 2048], P('pairs', None, 'tm')
Inputs may be any that keep to these rules, and one draw needn't show every extreme that they name: pair_blocks[p, k] names two different channel blocks; block j holds channels j * 128 to (j + 1) * 128 - 1. Owner p's pair blocks are its slots 0 to block_count[p] - 1; its later slots are empty and their rows of stacked are zero.
All inputs are finite; a program needn't handle non-finite values.
Results may differ from a plain program's by a relative error of at most 0.006.
Values may be sent and summed in bfloat16 or wider, within the bound.
No kernel may reach another device: no remote copies, remote signals or barrier semaphores. Data moves between devices by JAX's collectives and lax.ppermute only.
A program may use at most 128 MiB of HBM per device.

v0:
```python
import math

import jax
import jax.numpy as jnp
from jax import lax
from jax.sharding import PartitionSpec as P

C = 4096
CB = 128
NF = 1024
FIRST_BIN = 16
FFT_LEN = 8192
LAGS = 2048
SMOOTH = 32
MAXB = 4


amp_floor = 0.2


def extended_2(cells, sides, width):
    for axis, dim in sides:
        count = lax.axis_size(axis)
        ends = count - 1
        head = lax.slice_in_dim(cells, 0, width, axis=dim)
        tail = lax.slice_in_dim(cells, cells.shape[dim] - width, cells.shape[dim], axis=dim)
        cells = jnp.concatenate(
            [
                lax.ppermute(tail, axis, [(i, (i + 1) % count) for i in range(ends)]),
                cells,
                lax.ppermute(head, axis, [((i + 1) % count, i) for i in range(ends)]),
            ],
            axis=dim,
        )
    return cells


def whiten(raw_spectra):
    components = raw_spectra.astype(jnp.float32)
    magnitude = jnp.sqrt(components[0] * components[0] + components[1] * components[1])
    rank_total = magnitude.ndim
    window = (1, 2 * SMOOTH + 1) + (1,) * (rank_total - 2)
    padding = ((0, 0),) * rank_total
    inner_part = components[:, :, SMOOTH : components.shape[2] - SMOOTH]
    window_sum = lax.reduce_window(
        magnitude, jnp.zeros((), magnitude.dtype), lax.add, window, (1,) * rank_total, padding
    )
    smoothed = window_sum / (2 * SMOOTH + 1)
    return (inner_part / (smoothed[None] + 1e-05)).astype(jnp.bfloat16)


def lag_table(offset, span_width, bin_total):
    bin_index = lax.iota(jnp.int32, bin_total)[:, None] + FIRST_BIN
    lag_index = lax.iota(jnp.int32, span_width)[None, :] + offset + (FFT_LEN - LAGS // 2)
    phase_step = bin_index * lag_index % FFT_LEN
    phase_angle = phase_step.astype(jnp.float32) * (2.0 * math.pi / FFT_LEN)
    scale_factor = 1.0 / math.sqrt(bin_total)
    cosine = jnp.cos(phase_angle) * scale_factor
    sine_part = jnp.sin(phase_angle) * scale_factor
    real_rows = jnp.stack([cosine, sine_part], axis=1)
    imag_rows = jnp.stack([-sine_part, cosine], axis=1)
    return jnp.stack([real_rows, imag_rows], axis=0).astype(jnp.bfloat16)


def phase_stack(lagged):
    correlation = lagged[:, :, :, 0]
    quadrature = lagged[:, :, :, 1]
    linear = jnp.mean(correlation, axis=0)
    magnitude = jnp.sqrt(correlation * correlation + quadrature * quadrature)
    inverse = 1.0 / jnp.maximum(magnitude, amp_floor)
    mean_real = jnp.mean(correlation * inverse, axis=0)
    mean_imag = jnp.mean(quadrature * inverse, axis=0)
    return linear * (mean_real * mean_real + mean_imag * mean_imag)


def on_device(spectra, pair_blocks, block_count):
    owner_index = lax.axis_index("pairs")
    hours_here = spectra.shape[1]
    block_total = C // CB
    own_blocks = lax.dynamic_index_in_dim(pair_blocks, owner_index, 0, keepdims=False).reshape(
        2 * MAXB
    )
    live_count = lax.dynamic_index_in_dim(block_count, owner_index, 0, keepdims=False)
    extended = extended_2(spectra, (("pairs", 2),), SMOOTH)
    source = whiten(extended)
    blank_blocks = jnp.zeros((2, hours_here, NF, 2 * MAXB, CB), jnp.bfloat16)
    band_piece = lax.all_gather(source, "pairs", axis=2, tiled=True)
    band_rows = band_piece.shape[2]
    chosen = jnp.take(
        band_piece.reshape(2, hours_here, band_rows, block_total, CB), own_blocks, axis=3
    )
    gathered = lax.dynamic_update_slice_in_dim(blank_blocks, chosen, jnp.int32(0), 2)
    left_block = gathered[:, :, :, 0::2].astype(jnp.float32)
    right_block = gathered[:, :, :, 1::2].astype(jnp.float32)
    cross_real = left_block[0] * right_block[0] + left_block[1] * right_block[1]
    cross_imag = left_block[1] * right_block[0] - left_block[0] * right_block[1]
    cross_spectra = jnp.stack([cross_real, cross_imag]).astype(jnp.bfloat16)
    lag_block = min(256, LAGS)
    initial = jnp.zeros((hours_here, MAXB, CB, 2, LAGS), jnp.bfloat16)
    live_mask = (lax.iota(jnp.int32, MAXB) < live_count).astype(jnp.float32)

    def fill_lags(block_step, buffer):
        offset = block_step * lag_block
        inverse_table = lag_table(offset, lag_block, NF)
        partial_value = jnp.einsum(
            "chfkb,cfgl->hkbgl", cross_spectra, inverse_table, preferred_element_type=jnp.float32
        )
        partial_value = partial_value * live_mask[None, :, None, None, None]
        return lax.dynamic_update_slice_in_dim(
            buffer, partial_value.astype(jnp.bfloat16), offset, 4
        )

    lagged = lax.fori_loop(0, LAGS // lag_block, fill_lags, initial)
    regrouped = lax.all_to_all(lagged, "tm", split_axis=4, concat_axis=0, tiled=True)
    return phase_stack(regrouped.astype(jnp.float32))


def solution(mesh):
    return jax.shard_map(
        on_device,
        mesh=mesh,
        in_specs=(P(None, "tm", "pairs", None), P(), P()),
        out_specs=P("pairs", None, "tm"),
        check_vma=False,
    )
```

profile of v0, /device:TPU:8, one launch (start us, length us, event | category | flops | bytes accessed | tf_op | source)
XLA Modules:
  0.0 375.9 jit_solution(12951018659126411125)
XLA Ops:
  6.5 2.0 collective-permute-start
  8.6 3.6 collective-permute-start.1
  12.2 5.1 %collective-permute-done = bf16[2,1,32,4096]{3,2,1,0:T(8,128)(2,1)S(1)} collective-permute-done((bf16[2,1,32,4096]{3,2,1,0:T(8,128)(2,1)}, bf16[2,1,32,4096]{3,2,1,0:T(8,128)(2,1)S(1)}, u32[]{:S(2)}, u32[]{:S(2)}) %collective-permute-start) | collective-permute-done | bytes 524320 | tf_op jit(solution)/shard_map/ppermute | solution.py:29
  17.4 1.9 collective-permute-done.1
  19.2 1.4 maximum_convert_fusion
  20.6 1.7 fusion.30
  22.3 11.2 %reduce_window.10 = f32[32,4096]{1,0:T(8,128)} reduce-window(f32[96,4096]{1,0:T(8,128)} %fusion.30, f32[]{:T(128)} %constant.141.clone.1), window={size=65x1}, to_apply=%region_0.1 | reduce-window | flops 8388608 | bytes 2097156 | tf_op jit(solution)/shard_map/reduce_window | solution.py:45
  37.2 81.6 %all-gather.2.cloned.1.call-done = bf16[2,1,1024,4096]{3,0,1,2:T(2,128)(2,1)} async-done(((bf16[2,1,32,4096]{3,0,1,2:T(2,128)(2,1)}), bf16[2,1,1024,4096]{3,0,1,2:T(2,128)(2,1)}) %all-gather.2.cloned.1.call-update) | async-done | bytes 16777232 | tf_op jit(solution)/shard_map/all_gather | solution.py:87
  118.8 40.8 %copy.15 = bf16[2,1,1024,4096]{2,3,0,1:T(8,128)(2,1)} copy(bf16[2,1,1024,4096]{3,0,1,2:T(2,128)(2,1)} %all-gather.2.cloned.1.call-done) | data formatting | bytes 33554432 | tf_op jit(solution)/shard_map/all_gather | solution.py:87
  159.6 21.2 %copy.16 = bf16[2,1024,32,128]{3,1,2,0:T(8,128)(2,1)} copy(bf16[2,1024,32,128]{1,3,2,0:T(8,128)(2,1)} %bitcast.98) | data formatting | bytes 33554432 | tf_op jit(solution)/shard_map/reshape | solution.py:90
  180.8 8.8 %gather_fusion = bf16[8,2,1024,128]{3,2,1,0:T(8,128)(2,1)} fusion(bf16[2,1024,32,128]{3,1,2,0:T(8,128)(2,1)} %copy.16, s32[1024]{0:T(1024)S(1)} %pad_clamp_fusion), kind=kCustom, calls=%fused_computation | custom fusion | bytes 8388640 | tf_op jit(solution)/shard_map/jit(_take)/gather | solution.py:89
  189.6 2.7 bitcast_select_fusion
  193.9 2.9 broadcast_in_dim.23.clone
  196.8 63.9 %while.16 = (s32[]{:T(128)}, bf16[1,4,128,2,2048]{2,1,3,0,4:T(4,128)(2,1)}, bf16[2,1,1024,4,128]{4,2,0,3,1:T(8,128)(2,1)S(1)}, s32[]{:T(128)}, s32[]{:T(128)}, /*index=5*/s32[]{:T(128)}, s32[]{:T(128)}, s32[]{:T(128)}) while((s32[]{:T(128)}, bf16[1,4,128,2,2048]{2,1,3,0,4:T(4,128)(2,1)}, ...), condition=%wide.region_2.3_spmd.clone, body=%wide.region_1.2_spmd.clone.sunk | while | flops 1084753408 | bytes 11020463 | solution.py:113
  197.5 4.6 %fusion.37 = (bf16[1024,1,256]{0,2,1:T(8,128)(2,1)S(1)}, bf16[1024,1,256]{0,2,1:T(8,128)(2,1)S(1)}, bf16[1024,1,256]{0,2,1:T(8,128)(2,1)S(1)}) fusion(s32[256]{0:T(256)S(1)} %add_add_fusion.2, s32[1024]{0:T(1024)S(1)} %iota_add_fusion.2), kind=kLoop, calls=%fused_computation.24.clone.1 | loop fusion | flops 5242880 | bytes 1577984 | tf_op jit(solution)/shard_map/convert.7
  205.4 4.6 %fusion.37 = (bf16[1024,1,256]{0,2,1:T(8,128)(2,1)S(1)}, bf16[1024,1,256]{0,2,1:T(8,128)(2,1)S(1)}, bf16[1024,1,256]{0,2,1:T(8,128)(2,1)S(1)}) fusion(s32[256]{0:T(256)S(1)} %add_add_fusion.2, s32[1024]{0:T(1024)S(1)} %iota_add_fusion.2), kind=kLoop, calls=%fused_computation.24.clone.1 | loop fusion | flops 5242880 | bytes 1577984 | tf_op jit(solution)/shard_map/convert.7
  213.4 4.6 %fusion.37 = (bf16[1024,1,256]{0,2,1:T(8,128)(2,1)S(1)}, bf16[1024,1,256]{0,2,1:T(8,128)(2,1)S(1)}, bf16[1024,1,256]{0,2,1:T(8,128)(2,1)S(1)}) fusion(s32[256]{0:T(256)S(1)} %add_add_fusion.2, s32[1024]{0:T(1024)S(1)} %iota_add_fusion.2), kind=kLoop, calls=%fused_computation.24.clone.1 | loop fusion | flops 5242880 | bytes 1577984 | tf_op jit(solution)/shard_map/convert.7
  221.4 4.6 %fusion.37 = (bf16[1024,1,256]{0,2,1:T(8,128)(2,1)S(1)}, bf16[1024,1,256]{0,2,1:T(8,128)(2,1)S(1)}, bf16[1024,1,256]{0,2,1:T(8,128)(2,1)S(1)}) fusion(s32[256]{0:T(256)S(1)} %add_add_fusion.2, s32[1024]{0:T(1024)S(1)} %iota_add_fusion.2), kind=kLoop, calls=%fused_computation.24.clone.1 | loop fusion | flops 5242880 | bytes 1577984 | tf_op jit(solution)/shard_map/convert.7
  229.4 4.6 %fusion.37 = (bf16[1024,1,256]{0,2,1:T(8,128)(2,1)S(1)}, bf16[1024,1,256]{0,2,1:T(8,128)(2,1)S(1)}, bf16[1024,1,256]{0,2,1:T(8,128)(2,1)S(1)}) fusion(s32[256]{0:T(256)S(1)} %add_add_fusion.2, s32[1024]{0:T(1024)S(1)} %iota_add_fusion.2), kind=kLoop, calls=%fused_computation.24.clone.1 | loop fusion | flops 5242880 | bytes 1577984 | tf_op jit(solution)/shard_map/convert.7
  237.4 4.6 %fusion.37 = (bf16[1024,1,256]{0,2,1:T(8,128)(2,1)S(1)}, bf16[1024,1,256]{0,2,1:T(8,128)(2,1)S(1)}, bf16[1024,1,256]{0,2,1:T(8,128)(2,1)S(1)}) fusion(s32[256]{0:T(256)S(1)} %add_add_fusion.2, s32[1024]{0:T(1024)S(1)} %iota_add_fusion.2), kind=kLoop, calls=%fused_computation.24.clone.1 | loop fusion | flops 5242880 | bytes 1577984 | tf_op jit(solution)/shard_map/convert.7
  245.4 4.6 %fusion.37 = (bf16[1024,1,256]{0,2,1:T(8,128)(2,1)S(1)}, bf16[1024,1,256]{0,2,1:T(8,128)(2,1)S(1)}, bf16[1024,1,256]{0,2,1:T(8,128)(2,1)S(1)}) fusion(s32[256]{0:T(256)S(1)} %add_add_fusion.2, s32[1024]{0:T(1024)S(1)} %iota_add_fusion.2), kind=kLoop, calls=%fused_computation.24.clone.1 | loop fusion | flops 5242880 | bytes 1577984 | tf_op jit(solution)/shard_map/convert.7
  253.4 4.6 %fusion.37 = (bf16[1024,1,256]{0,2,1:T(8,128)(2,1)S(1)}, bf16[1024,1,256]{0,2,1:T(8,128)(2,1)S(1)}, bf16[1024,1,256]{0,2,1:T(8,128)(2,1)S(1)}) fusion(s32[256]{0:T(256)S(1)} %add_add_fusion.2, s32[1024]{0:T(1024)S(1)} %iota_add_fusion.2), kind=kLoop, calls=%fused_computation.24.clone.1 | loop fusion | flops 5242880 | bytes 1577984 | tf_op jit(solution)/shard_map/convert.7
  260.7 103.6 %all_to_all.4 = bf16[1,4,128,2,2048]{2,1,3,0,4:T(4,128)(2,1)S(1)} all-to-all(bf16[1,4,128,2,2048]{2,1,3,0,4:T(4,128)(2,1)} %get-tuple-element.116), channel_id=1, replica_groups=mesh['pairs'=32,'tm'=8] {'tm'}, dimensions={4} | all-to-all | bytes 8388608 | tf_op jit(solution)/shard_map/all_to_all | solution.py:114
  365.6 2.3 fusion.27
  (73 shorter events, 34.4 us)
Async XLA Ops:
  6.5 29.6 %copy-start = (s32[32,4,2]{0,2,1:T(2,128)S(1)}, s32[32,4,2]{0,2,1:T(2,128)}, u32[]{:S(2)}) copy-start(s32[32,4,2]{0,2,1:T(2,128)} %param.6) | copy-start | bytes 3076
  6.5 112.3 %all-gather.2.cloned.1.call-start = ((), (), s32[]{:S(2)}) async-start(), calls=%async_computation.1 | async-start | bytes 17301504 | tf_op jit(solution)/shard_map/all_gather | solution.py:87
  6.5 10.8 %collective-permute-start = (bf16[2,1,32,4096]{3,2,1,0:T(8,128)(2,1)}, bf16[2,1,32,4096]{3,2,1,0:T(8,128)(2,1)S(1)}, u32[]{:S(2)}, u32[]{:S(2)}) collective-permute-start(bf16[2,1,32,4096]{3,2,1,0:T(8,128)(2,1)} %param.5), channel_id=1, source_target_pairs={{0,8},{8,16},{16,24},{24,32},{32,40},{40,48},{48,56},{56,64},{64,7... | collective-permute-start | bytes 1572872 | tf_op jit(solution)/shard_map/ppermute | solution.py:29
  8.6 10.6 %collective-permute-start.1 = (bf16[2,1,32,4096]{3,2,1,0:T(8,128)(2,1)}, bf16[2,1,32,4096]{3,2,1,0:T(8,128)(2,1)S(1)}, u32[]{:S(2)}, u32[]{:S(2)}) collective-permute-start(bf16[2,1,32,4096]{3,2,1,0:T(8,128)(2,1)} %param.5), channel_id=1, source_target_pairs={{8,0},{16,8},{24,16},{32,24},{40,32},{48,40},{56,48},{64,56},{72,6... | collective-permute-start | bytes 1572872 | tf_op jit(solution)/shard_map/ppermute | solution.py:31
  22.3 14.2 %copy-start.2 = (s32[32]{0:T(128)S(1)}, s32[32]{0:T(128)}, u32[]{:S(2)}) copy-start(s32[32]{0:T(128)} %param.7) | copy-start | bytes 388
  365.3 3.7 copy-start.1
Sparse Core Ops, SparseCore 0:
  36.2 82.5 all-gather.1
where the time goes:
time: 379 us; the launch traced here: 376 us
  blocking collectives  104 us (27%)
  waiting for transfers between devices  88.6 us (23%)
  local copies, waits for them, and re-layouts  87.8 us (23%)
  other arithmetic  66.2 us (17%)
  between operations  13.5 us (4%)
  matrix products  10.1 us (3%)
  starting transfers between devices  5.68 us (1%)
    all_to_all x1, blocking collectives, on_device(): lax.all_to_all(lagged, 'tm', split_axis=4, concat_axis=0, tiled=True)  104 us
    all_gather x1, waiting for transfers between devices, on_device(): band_piece = lax.all_gather(source, 'pairs', axis=2, tiled=True)  81.6 us
    all_gather x1, local copies, waits for them, and re-layouts, on_device(): band_piece = lax.all_gather(source, 'pairs', axis=2, tiled=True)  40.8 us
    another operation x9, other arithmetic  37.4 us
    reshape x1, local copies, waits for them, and re-layouts, on_device(): band_piece.reshape(2, hours_here, band_rows, block_total, CB)  21.2 us
    another operation x2, other arithmetic, whiten(): lax.reduce_window(magnitude, jnp.zeros((), magnitude.dtype), lax.add, win...  12.9 us
    dot_general x8, matrix products, fill_lags(): jnp.einsum('chfkb,cfgl->hkbgl', cross_spectra, inverse_table, preferred_e...  10.1 us
    dynamic_update_slice x8, local copies, waits for them, and re-layouts, fill_lags(): lax.dynamic_update_slice_in_dim(buffer, partial_value.astype(jnp.bfloat16...  9.74 us
  transfers between devices with their start and end apart: 3, of which 3 were waited for; matrix products, arithmetic and copies ran while one was open for 0% of the time, Pallas kernels for 0%

commit v1 on v0

v1 whole, which is shorter than its diff:
```python
import functools
import math

import jax
import jax.numpy as jnp
import ml_dtypes
import numpy as np
from jax import lax
from jax.experimental import pallas as pl
from jax.experimental.pallas import tpu as pltpu
from jax.sharding import PartitionSpec as P

C = 4096
CB = 128
NF = 1024
FIRST_BIN = 16
FFT_LEN = 8192
LAGS = 2048
SMOOTH = 32
MAXB = 4
HOURS = 8
OWNERS = 32
amp_floor = 0.2

CHIPS = OWNERS // 2
BINS = NF // OWNERS
CHIP_BINS = 2 * BINS
LAG_PART = LAGS // HOURS
RANK_CHIP = 28
RANK_PART = 48
ROWS_CHIP = 2 * RANK_CHIP
ROWS_PART = 2 * RANK_PART
STEP = 2.0 * math.pi / FFT_LEN


def slepian(points, half_width, count):
    n = np.arange(points, dtype=np.float64)
    tri = np.diag(((points - 1) / 2.0 - n) ** 2 * math.cos(2.0 * math.pi * half_width))
    off = n[1:] * (points - n[1:]) / 2.0
    tri = tri + np.diag(off, 1) + np.diag(off, -1)
    vectors = np.linalg.eigh(tri)[1][:, ::-1][:, :count]
    return vectors * np.where(vectors[points // 2] < 0, -1.0, 1.0)


def split_rounded(table):
    high = table.astype(ml_dtypes.bfloat16)
    low = (table - high.astype(np.float64)).astype(ml_dtypes.bfloat16)
    return high, low


def real_form(table):
    return np.block([[table.real, -table.imag], [table.imag, table.real]])


@functools.cache
def tables():
    chip_basis = slepian(CHIP_BINS, LAGS / 2 / FFT_LEN, RANK_CHIP)
    part_basis = slepian(NF, LAG_PART / 2 / FFT_LEN, RANK_PART)
    bins = np.arange(NF) - (NF - 1) / 2.0
    lags = np.arange(LAG_PART) - (LAG_PART - 1) / 2.0
    mid_bin = FIRST_BIN + (NF - 1) / 2.0
    compress = np.kron(np.eye(2), chip_basis.T)
    parts = []
    for part in range(HOURS):
        mid_lag = LAG_PART * part - LAGS // 2 + (LAG_PART - 1) / 2.0
        turned = np.exp(1j * STEP * (bins + mid_bin) * mid_lag)[:, None] * part_basis
        turned = turned.reshape(CHIPS, CHIP_BINS, RANK_PART)
        blocks = [real_form((chip_basis.T @ turned[chip]).T) for chip in range(CHIPS)]
        parts.append(np.concatenate(blocks, axis=1))
    combine = np.concatenate(parts, axis=0)
    waves = np.exp(1j * STEP * np.outer(lags, bins)) @ part_basis
    waves = waves * np.exp(1j * STEP * mid_bin * lags)[:, None] / math.sqrt(NF)
    expand = real_form(waves)
    row = np.arange(CHIP_BINS)[:, None] + SMOOTH
    column = np.arange(CHIP_BINS + 2 * SMOOTH)[None, :]
    window = (np.abs(row - column) <= SMOOTH).astype(ml_dtypes.bfloat16)
    compress = np.concatenate(split_rounded(compress), axis=1)
    expand = np.concatenate(split_rounded(expand), axis=1)
    return window, compress, split_rounded(combine), expand


def magnitude_of(real, imag):
    return jnp.sqrt(real * real + imag * imag)


def cross_kernel(
    blocks, core_ref, own, twin, near, far, window, compress, out, magnitudes, white, columns
):
    core = core_ref[0]
    own_row = pl.multiple_of(core * BINS, BINS)
    twin_row = pl.multiple_of((1 - core) * BINS, BINS)
    near_row = pl.multiple_of(core * (CHIP_BINS + SMOOTH), BINS)
    far_row = pl.multiple_of((1 - core) * (CHIP_BINS + SMOOTH), BINS)
    chunk = 512

    def whiten(step, carry):
        lanes = pl.ds(pl.multiple_of(step * chunk, chunk), chunk)
        magnitudes[pl.ds(near_row, SMOOTH), :] = near[:, lanes]
        magnitudes[pl.ds(far_row, SMOOTH), :] = far[:, lanes]
        parts = []
        for source, first in ((own, own_row), (twin, twin_row)):
            real = source[0, :, lanes].astype(jnp.float32)
            imag = source[1, :, lanes].astype(jnp.float32)
            size = magnitude_of(real, imag).astype(jnp.bfloat16)
            magnitudes[pl.ds(pl.multiple_of(first + SMOOTH, BINS), BINS), :] = size
            parts.append((real, imag, first))
        sums = jnp.dot(window[...], magnitudes[...], preferred_element_type=jnp.float32)
        smoothed = sums * (1.0 / (2 * SMOOTH + 1))
        columns[:, :chunk] = 1.0 / (smoothed + 1e-05)
        for real, imag, first in parts:
            inverse = columns[pl.ds(first, BINS), :chunk]
            white[0, pl.ds(first, BINS), lanes] = (real * inverse).astype(jnp.bfloat16)
            white[1, pl.ds(first, BINS), lanes] = (imag * inverse).astype(jnp.bfloat16)
        return carry

    lax.fori_loop(0, C // chunk, whiten, 0)

    def one_owner(chip, carry):
        base = (2 * chip + core) * (2 * MAXB)
        crossed = []
        for slot in range(MAXB):
            left = pl.ds(pl.multiple_of(blocks[base + 2 * slot] * CB, CB), CB)
            right = pl.ds(pl.multiple_of(blocks[base + 2 * slot + 1] * CB, CB), CB)
            left_re = white[0, :, left].astype(jnp.float32)
            left_im = white[1, :, left].astype(jnp.float32)
            right_re = white[0, :, right].astype(jnp.float32)
            right_im = white[1, :, right].astype(jnp.float32)
            real = left_re * right_re + left_im * right_im
            imag = left_im * right_re - left_re * right_im
            crossed.append(jnp.concatenate([real, imag], axis=0).astype(jnp.bfloat16))
        cross = jnp.concatenate(crossed, axis=1)
        cross = jnp.concatenate([cross, cross], axis=0)
        packed = jnp.dot(compress[...], cross, preferred_element_type=jnp.float32)
        out[chip] = packed.astype(jnp.bfloat16)
        return carry

    lax.fori_loop(0, CHIPS, one_owner, 0)


def combine_kernel(high, low, packed, out):
    value = packed[...]
    total = jnp.dot(high[...], value, preferred_element_type=jnp.float32)
    total = total + jnp.dot(low[...], value, preferred_element_type=jnp.float32)
    out[...] = total.astype(jnp.bfloat16)


def stack_kernel(live_ref, expand, parts, out):
    step = pl.program_id(0)
    linear = mean_real = mean_imag = None
    for hour in range(HOURS):
        part = parts[hour]
        part = jnp.concatenate([part, part], axis=0)
        lagged = jnp.dot(expand[...], part, preferred_element_type=jnp.float32)
        correlation = lagged[:LAG_PART]
        quadrature = lagged[LAG_PART:]
        power = correlation * correlation + quadrature * quadrature
        inverse = jnp.minimum(lax.rsqrt(power), 1.0 / amp_floor)
        unit_real = correlation * inverse
        unit_imag = quadrature * inverse
        if hour == 0:
            linear, mean_real, mean_imag = correlation, unit_real, unit_imag
        else:
            linear = linear + correlation
            mean_real = mean_real + unit_real
            mean_imag = mean_imag + unit_imag
    stacked = linear * (mean_real * mean_real + mean_imag * mean_imag) * (1.0 / HOURS**3)
    turned = stacked.T
    slots = out.shape[0]
    for slot in range(slots):
        live = step * slots + slot < live_ref[0]
        piece = turned[slot * CB : (slot + 1) * CB]
        out[slot] = jnp.where(live, piece, jnp.zeros_like(piece))


def on_device(spectra, pair_blocks, block_count):
    owner = lax.axis_index("pairs")
    core = owner % 2
    window, compress, (high, low), expand = tables()
    spectra = spectra[:, 0]
    wide = spectra.astype(jnp.float32)
    magnitude = magnitude_of(wide[0], wide[1]).astype(jnp.bfloat16)
    twin = lax.ppermute(spectra, "pairs", [(i, i ^ 1) for i in range(OWNERS)])
    last = OWNERS - 1
    near_pairs = [(i, i + 1) for i in range(1, last, 2)] + [(i, i - 1) for i in range(2, last, 2)]
    far_pairs = [(i, i + 2) for i in range(1, last - 1, 2)] + [(i, i - 2) for i in range(2, last, 2)]
    near = lax.ppermute(magnitude, "pairs", near_pairs)
    far = lax.ppermute(magnitude, "pairs", far_pairs)
    vmem = pl.BlockSpec(memory_space=pltpu.VMEM)
    smem = pl.BlockSpec(memory_space=pltpu.SMEM)
    packed = pl.pallas_call(
        cross_kernel,
        out_shape=jax.ShapeDtypeStruct((CHIPS, ROWS_CHIP, MAXB * CB), jnp.bfloat16),
        in_specs=[smem, smem] + [vmem] * 6,
        out_specs=vmem,
        scratch_shapes=[
            pltpu.VMEM((CHIP_BINS + 2 * SMOOTH, 512), jnp.bfloat16),
            pltpu.VMEM((2, CHIP_BINS, C), jnp.bfloat16),
            pltpu.VMEM((CHIP_BINS, 512), jnp.float32),
        ],
        compiler_params=pltpu.CompilerParams(vmem_limit_bytes=32 * 2**20),
        name="cross",
    )(pair_blocks.reshape(-1), core[None], spectra, twin, near, far, window, compress)
    groups = [list(range(0, OWNERS, 2)), list(range(1, OWNERS, 2))]
    packed = lax.all_to_all(packed, "pairs", 0, 0, axis_index_groups=groups, tiled=True)
    packed = packed.reshape(CHIPS * ROWS_CHIP, MAXB * CB)
    parts = pl.pallas_call(
        combine_kernel,
        out_shape=jax.ShapeDtypeStruct((HOURS * ROWS_PART, MAXB * CB), jnp.bfloat16),
        in_specs=[vmem] * 3,
        out_specs=vmem,
        compiler_params=pltpu.CompilerParams(vmem_limit_bytes=32 * 2**20),
        name="combine",
    )(high, low, packed)
    parts = parts.reshape(HOURS, ROWS_PART, MAXB * CB)
    parts = lax.all_to_all(parts, "tm", 0, 0, tiled=True)
    live = lax.dynamic_index_in_dim(block_count, owner, 0, keepdims=True)
    slots = 2
    return pl.pallas_call(
        stack_kernel,
        grid=(MAXB // slots,),
        out_shape=jax.ShapeDtypeStruct((MAXB, CB, LAG_PART), jnp.float32),
        in_specs=[
            smem,
            pl.BlockSpec((2 * LAG_PART, 2 * ROWS_PART), lambda i: (0, 0)),
            pl.BlockSpec((HOURS, ROWS_PART, slots * CB), lambda i: (0, 0, i)),
        ],
        out_specs=pl.BlockSpec((slots, CB, LAG_PART), lambda i: (i, 0, 0)),
        compiler_params=pltpu.CompilerParams(vmem_limit_bytes=32 * 2**20),
        name="stack",
    )(live, expand, parts)


def solution(mesh):
    return jax.shard_map(
        on_device,
        mesh=mesh,
        in_specs=(P(None, "tm", "pairs", None), P(), P()),
        out_specs=P("pairs", None, "tm"),
        check_vma=False,
    )
```

time: 379 us -> 80.1 us (0.21)
  local copies, waits for them, and re-layouts: 87.8 us -> 0.86 us
  blocking collectives: 104 us -> 22.7 us
  other arithmetic: 66.2 us -> 1.38 us
  waiting for transfers between devices: 88.6 us -> 27.2 us
  between operations: 13.5 us -> 0.12 us
  Pallas kernels: 0 us -> 12.5 us
  matrix products: 10.1 us -> 0 us
  starting transfers between devices: 5.68 us -> 14.7 us
    all_gather x1 -> x0, waiting for transfers between devices: 81.6 us -> none  [on_device(): band_piece = lax.all_gather(source, 'pairs', axis=2, tiled=True)]
    all_to_all x1, blocking collectives: 104 us -> 22.7 us  [on_device(): lax.all_to_all(packed, 'pairs', 0, 0, axis_index_groups=groups, tiled=True)]
    another operation x20 -> x0, other arithmetic: 51.9 us -> none
    all_gather x1 -> x0, local copies, waits for them, and re-layouts: 40.8 us -> none  [on_device(): band_piece = lax.all_gather(source, 'pairs', axis=2, tiled=True)]
    all_to_all x0 -> x1, waiting for transfers between devices: none -> 21.8 us  [on_device(): parts = lax.all_to_all(parts, 'tm', 0, 0, tiled=True)]
    reshape x3 -> x1, local copies, waits for them, and re-layouts: 21.4 us -> 0.15 us  [on_device(): pair_blocks.reshape(-1)]
    pallas_call x0 -> x3, Pallas kernels: none -> 12.5 us  [the longest x1 6.27 us: on_device(): pl.pallas_call(cross_kernel, out_shape=jax.ShapeDtypeStruct((CHIPS, ROWS_...]
    dot_general x8 -> x0, matrix products: 10.1 us -> none  [fill_lags(): jnp.einsum('chfkb,cfgl->hkbgl', cross_spectra, inverse_table, preferred_e...]
  transfers between devices with their start and end apart: 3 -> 4, of which waited for: 3 -> 3; matrix products, arithmetic and copies ran while one was open for 0% -> 3% of each run, Pallas kernels for 0% -> 0%
where the time goes in v1:
time: 80.1 us; the launch traced here: 79.5 us
  waiting for transfers between devices  27.2 us (34%)
  blocking collectives  22.7 us (28%)
  starting transfers between devices  14.7 us (18%)
  Pallas kernels  12.5 us (16%)
  other arithmetic  1.38 us (2%)
  local copies, waits for them, and re-layouts  0.86 us (1%)
    all_to_all x1, blocking collectives, on_device(): lax.all_to_all(packed, 'pairs', 0, 0, axis_index_groups=groups, tiled=True)  22.7 us
    all_to_all x1, waiting for transfers between devices, on_device(): parts = lax.all_to_all(parts, 'tm', 0, 0, tiled=True)  21.8 us
    all_to_all x1, starting transfers between devices, on_device(): parts = lax.all_to_all(parts, 'tm', 0, 0, tiled=True)  8.59 us
    pallas_call x1, Pallas kernels, on_device(): pl.pallas_call(cross_kernel, out_shape=jax.ShapeDtypeStruct((CHIPS, ROWS_...  6.27 us
    ppermute x1, starting transfers between devices, on_device(): far = lax.ppermute(magnitude, 'pairs', far_pairs)  4.06 us
    pallas_call x1, Pallas kernels, on_device(): pl.pallas_call(stack_kernel, grid=(MAXB // slots,), out_shape=jax.ShapeDt...  3.61 us
    ppermute x1, waiting for transfers between devices, on_device(): near = lax.ppermute(magnitude, 'pairs', near_pairs)  3.49 us
    pallas_call x1, Pallas kernels, on_device(): pl.pallas_call(combine_kernel, out_shape=jax.ShapeDtypeStruct((HOURS * RO...  2.67 us
  transfers between devices with their start and end apart: 4, of which 3 were waited for; matrix products, arithmetic and copies ran while one was open for 3% of the time, Pallas kernels for 0%

profile of v1, /device:TPU:8, one launch (start us, length us, event | category | flops | bytes accessed | tf_op | source)
XLA Modules:
  0.0 79.5 jit_solution(7243818674002630876)
XLA Ops:
  0.0 0.0 copy-start.5
  0.0 0.1 collective-permute-start
  0.1 1.2 %bitcast_convert_fusion = f32[2,32,4096]{2,1,0:T(8,128)S(1)} fusion(bf16[2,1,32,4096]{3,2,1,0:T(8,128)(2,1)} %param.8), kind=kLoop, calls=%fused_computation.6 | loop fusion | flops 262144 | bytes 1572864 | tf_op jit(solution)/shard_map/convert_element_type | solution.py:180
  1.3 0.2 fusion.3
  1.5 4.1 %collective-permute-start.2 = (bf16[32,4096]{1,0:T(8,128)(2,1)S(1)}, bf16[32,4096]{1,0:T(8,128)(2,1)S(1)}, u32[]{:S(2)}, u32[]{:S(2)}) collective-permute-start(bf16[32,4096]{1,0:T(8,128)(2,1)S(1)} %fusion.3), channel_id=1, source_target_pairs={{8,24},{24,40},{40,56},{56,72},{72,88},{88,104},{104,120},{120,136... | collective-permute-start | bytes 786440 | tf_op jit(solution)/shard_map/ppermute | solution.py:187
  5.6 1.9 %collective-permute-start.1 = (bf16[32,4096]{1,0:T(8,128)(2,1)S(1)}, bf16[32,4096]{1,0:T(8,128)(2,1)S(1)}, u32[]{:S(2)}, u32[]{:S(2)}) collective-permute-start(bf16[32,4096]{1,0:T(8,128)(2,1)S(1)} %fusion.3), channel_id=1, source_target_pairs={{8,16},{24,32},{40,48},{56,64},{72,80},{88,96},{104,112},{120,128}... | collective-permute-start | bytes 786440 | tf_op jit(solution)/shard_map/ppermute | solution.py:186
  7.5 0.0 copy-done.6
  7.5 0.1 copy.9
  7.6 0.1 reshape.14.blocks
  7.8 2.0 %collective-permute-done.2.far = bf16[32,4096]{1,0:T(8,128)(2,1)S(1)} collective-permute-done((bf16[32,4096]{1,0:T(8,128)(2,1)S(1)}, bf16[32,4096]{1,0:T(8,128)(2,1)S(1)}, u32[]{:S(2)}, u32[]{:S(2)}) %collective-permute-start.2) | collective-permute-done | bytes 262176 | tf_op jit(solution)/shard_map/ppermute | solution.py:187
  9.8 3.5 %collective-permute-done.1.near = bf16[32,4096]{1,0:T(8,128)(2,1)S(1)} collective-permute-done((bf16[32,4096]{1,0:T(8,128)(2,1)S(1)}, bf16[32,4096]{1,0:T(8,128)(2,1)S(1)}, u32[]{:S(2)}, u32[]{:S(2)}) %collective-permute-start.1) | collective-permute-done | bytes 262176 | tf_op jit(solution)/shard_map/ppermute | solution.py:186
  13.3 0.0 collective-permute-done.twin
  13.3 0.0 copy-done
  13.3 0.0 copy-done.4
  13.3 0.0 copy-start.2
  13.3 6.3 %cross.1 = bf16[16,56,512]{2,1,0:T(8,128)(2,1)S(1)} custom-call(s32[256]{0:T(256)S(1)} %reshape.14.blocks, s32[1]{0:T(128)} %bitcast.core_ref, bf16[2,32,4096]{2,1,0:T(8,128)(2,1)S(1)} %bitcast.9, bf16[2,32,4096]{2,1,0:T(8,128)(2,1)S(1)} %collective-permute-done.twin, bf16[32,4096]{1,0:T(8,128)(2,1)S(1)} %collective-permute-done.1.near, ...), custom_call_target="tpu_custom_call" | custom-call | tf_op jit(solution)/shard_map/cross/pallas_call | solution.py:190
  19.6 0.0 copy-start.1
  19.6 22.7 %all_to_all.10 = bf16[16,56,512]{2,1,0:T(8,128)(2,1)S(1)} all-to-all(bf16[16,56,512]{2,1,0:T(8,128)(2,1)S(1)} %cross.1), channel_id=1, replica_groups={{0,16,32,48,64,80,96,112,128,144,160,176,192,208,224,240},{8,24,40,56,7..., dimensions={0} | all-to-all | bytes 1835008 | tf_op jit(solution)/shard_map/all_to_all | solution.py:204
  42.3 2.7 %combine.1 = bf16[768,512]{1,0:T(8,128)(2,1)} custom-call(bf16[768,896]{1,0:T(8,128)(2,1)S(1)} %copy-done.2, bf16[768,896]{1,0:T(8,128)(2,1)S(1)} %copy-done.1, bf16[896,512]{1,0:T(8,128)(2,1)S(1)} %bitcast.7), custom_call_target="tpu_custom_call" | custom-call | tf_op jit(solution)/shard_map/combine/pallas_call | solution.py:206
  44.9 8.6 %all-to-all-start.1 = ((bf16[8,96,512]{2,1,0:T(8,128)(2,1)}), bf16[8,96,512]{2,1,0:T(8,128)(2,1)S(1)}, u32[]{:S(2)}, u32[]{:S(2)}) async-start(bf16[8,96,512]{2,1,0:T(8,128)(2,1)} %bitcast.4), calls=%async_computation.1 | async-start | bytes 1572864 | tf_op jit(solution)/shard_map/all_to_all | solution.py:215
  53.5 0.6 dynamic_slice.4.live_ref
  54.1 21.8 %all-to-all-done.1.parts = bf16[8,96,512]{2,1,0:T(8,128)(2,1)S(1)} async-done(((bf16[8,96,512]{2,1,0:T(8,128)(2,1)}), bf16[8,96,512]{2,1,0:T(8,128)(2,1)S(1)}, u32[]{:S(2)}, u32[]{:S(2)}) %all-to-all-start.1) | async-done | bytes 786464 | tf_op jit(solution)/shard_map/all_to_all | solution.py:215
  75.9 0.0 copy-done.3
  75.9 3.6 %stack.1 = f32[4,128,256]{2,1,0:T(8,128)} custom-call(s32[1]{0:T(128)} %dynamic_slice.4.live_ref, bf16[512,192]{1,0:T(8,128)(2,1)S(1)} %copy-done.3, bf16[8,96,512]{2,1,0:T(8,128)(2,1)S(1)} %all-to-all-done.1.parts), custom_call_target="tpu_custom_call" | custom-call | tf_op jit(solution)/shard_map/stack/pallas_call | solution.py:218
  (9 shorter events, 0.0 us)
Async XLA Ops:
  0.0 7.5 %copy-start.6 = (s32[32,4,2]{0,2,1:T(2,128)S(1)}, s32[32,4,2]{0,2,1:T(2,128)}, u32[]{:S(2)}) copy-start(s32[32,4,2]{0,2,1:T(2,128)} %param.9) | copy-start | bytes 3076
  0.0 13.3 %copy-start = (bf16[2,1,32,4096]{3,2,1,0:T(8,128)(2,1)S(1)}, bf16[2,1,32,4096]{3,2,1,0:T(8,128)(2,1)}, u32[]{:S(2)}) copy-start(bf16[2,1,32,4096]{3,2,1,0:T(8,128)(2,1)} %param.8) | copy-start | bytes 1572868
  0.0 13.3 %copy-start.4 = (bf16[56,256]{1,0:T(8,128)(2,1)S(1)}, bf16[56,256]{1,0:T(8,128)(2,1)}, u32[]{:S(2)}) copy-start(bf16[56,256]{1,0:T(8,128)(2,1)} %constant.35.clone.compress) | copy-start | bytes 86020
  0.0 13.3 %copy-start.5 = (bf16[64,128]{1,0:T(8,128)(2,1)S(1)}, bf16[64,128]{1,0:T(8,128)(2,1)}, u32[]{:S(2)}) copy-start(bf16[64,128]{1,0:T(8,128)(2,1)} %constant.34.clone.window) | copy-start | bytes 49156
  0.0 13.2 %collective-permute-start = (bf16[2,32,4096]{2,1,0:T(8,128)(2,1)}, bf16[2,32,4096]{2,1,0:T(8,128)(2,1)S(1)}, u32[]{:S(2)}, u32[]{:S(2)}) collective-permute-start(bf16[2,32,4096]{2,1,0:T(8,128)(2,1)} %bitcast.8), channel_id=1, source_target_pairs={{0,8},{8,0},{16,24},{24,16},{32,40},{40,32},{48,56},{56,48},{64,72... | collective-permute-start | bytes 1572872 | tf_op jit(solution)/shard_map/ppermute | solution.py:182
  1.5 8.3 %collective-permute-start.2 = (bf16[32,4096]{1,0:T(8,128)(2,1)S(1)}, bf16[32,4096]{1,0:T(8,128)(2,1)S(1)}, u32[]{:S(2)}, u32[]{:S(2)}) collective-permute-start(bf16[32,4096]{1,0:T(8,128)(2,1)S(1)} %fusion.3), channel_id=1, source_target_pairs={{8,24},{24,40},{40,56},{56,72},{72,88},{88,104},{104,120},{120,136... | collective-permute-start | bytes 786440 | tf_op jit(solution)/shard_map/ppermute | solution.py:187
  5.6 7.7 %collective-permute-start.1 = (bf16[32,4096]{1,0:T(8,128)(2,1)S(1)}, bf16[32,4096]{1,0:T(8,128)(2,1)S(1)}, u32[]{:S(2)}, u32[]{:S(2)}) collective-permute-start(bf16[32,4096]{1,0:T(8,128)(2,1)S(1)} %fusion.3), channel_id=1, source_target_pairs={{8,16},{24,32},{40,48},{56,64},{72,80},{88,96},{104,112},{120,128}... | collective-permute-start | bytes 786440 | tf_op jit(solution)/shard_map/ppermute | solution.py:186
  13.3 29.0 %copy-start.2 = (bf16[768,896]{1,0:T(8,128)(2,1)S(1)}, bf16[768,896]{1,0:T(8,128)(2,1)}, u32[]{:S(2)}) copy-start(bf16[768,896]{1,0:T(8,128)(2,1)} %constant.36.clone.high) | copy-start | bytes 4128772
  19.6 22.7 %copy-start.1 = (bf16[768,896]{1,0:T(8,128)(2,1)S(1)}, bf16[768,896]{1,0:T(8,128)(2,1)}, u32[]{:S(2)}) copy-start(bf16[768,896]{1,0:T(8,128)(2,1)} %constant.37.clone.low) | copy-start | bytes 4128772
  44.9 8.6 %copy-start.7 = (s32[32]{0:T(128)S(1)}, s32[32]{0:T(128)}, u32[]{:S(2)}) copy-start(s32[32]{0:T(128)} %param.10) | copy-start | bytes 388
  44.9 30.9 %copy-start.3 = (bf16[512,192]{1,0:T(8,128)(2,1)S(1)}, bf16[512,192]{1,0:T(8,128)(2,1)}, u32[]{:S(2)}) copy-start(bf16[512,192]{1,0:T(8,128)(2,1)} %constant.38.clone.expand) | copy-start | bytes 589828
  44.9 30.9 %all-to-all-start.1 = ((bf16[8,96,512]{2,1,0:T(8,128)(2,1)}), bf16[8,96,512]{2,1,0:T(8,128)(2,1)S(1)}, u32[]{:S(2)}, u32[]{:S(2)}) async-start(bf16[8,96,512]{2,1,0:T(8,128)(2,1)} %bitcast.4), calls=%async_computation.1 | async-start | bytes 1572864 | tf_op jit(solution)/shard_map/all_to_all | solution.py:215

commit v2 on v1

--- a/solution.py
+++ b/solution.py
@@ -75,7 +75,7 @@
     column = np.arange(CHIP_BINS + 2 * SMOOTH)[None, :]
     window = (np.abs(row - column) <= SMOOTH).astype(ml_dtypes.bfloat16)
     compress = np.concatenate(split_rounded(compress), axis=1)
-    expand = np.concatenate(split_rounded(expand), axis=1)
+    expand = np.ascontiguousarray(np.concatenate(split_rounded(expand), axis=1).T)
     return window, compress, split_rounded(combine), expand
 
 
@@ -113,7 +113,7 @@
             white[1, pl.ds(first, BINS), lanes] = (imag * inverse).astype(jnp.bfloat16)
         return carry
 
-    lax.fori_loop(0, C // chunk, whiten, 0)
+    lax.fori_loop(0, C // chunk, whiten, 0, unroll=True)
 
     def one_owner(chip, carry):
         base = (2 * chip + core) * (2 * MAXB)
@@ -134,7 +134,7 @@
         out[chip] = packed.astype(jnp.bfloat16)
         return carry
 
-    lax.fori_loop(0, CHIPS, one_owner, 0)
+    lax.fori_loop(0, CHIPS, one_owner, 0, unroll=True)
 
 
 def combine_kernel(high, low, packed, out):
@@ -146,30 +146,30 @@
 
 def stack_kernel(live_ref, expand, parts, out):
     step = pl.program_id(0)
-    linear = mean_real = mean_imag = None
-    for hour in range(HOURS):
-        part = parts[hour]
-        part = jnp.concatenate([part, part], axis=0)
-        lagged = jnp.dot(expand[...], part, preferred_element_type=jnp.float32)
-        correlation = lagged[:LAG_PART]
-        quadrature = lagged[LAG_PART:]
-        power = correlation * correlation + quadrature * quadrature
-        inverse = jnp.minimum(lax.rsqrt(power), 1.0 / amp_floor)
-        unit_real = correlation * inverse
-        unit_imag = quadrature * inverse
-        if hour == 0:
-            linear, mean_real, mean_imag = correlation, unit_real, unit_imag
-        else:
-            linear = linear + correlation
-            mean_real = mean_real + unit_real
-            mean_imag = mean_imag + unit_imag
-    stacked = linear * (mean_real * mean_real + mean_imag * mean_imag) * (1.0 / HOURS**3)
-    turned = stacked.T
-    slots = out.shape[0]
-    for slot in range(slots):
-        live = step * slots + slot < live_ref[0]
-        piece = turned[slot * CB : (slot + 1) * CB]
-        out[slot] = jnp.where(live, piece, jnp.zeros_like(piece))
+    for slot in range(out.shape[0]):
+        lanes = slice(slot * CB, (slot + 1) * CB)
+        linear = mean_real = mean_imag = None
+        for hour in range(HOURS):
+            part = parts[hour, :, lanes]
+            part = jnp.concatenate([part, part], axis=0)
+            lagged = lax.dot_general(
+                part, expand[...], (((0,), (0,)), ((), ())), preferred_element_type=jnp.float32
+            )
+            correlation = lagged[:, :LAG_PART]
+            quadrature = lagged[:, LAG_PART:]
+            power = correlation * correlation + quadrature * quadrature
+            inverse = jnp.minimum(lax.rsqrt(power), 1.0 / amp_floor)
+            unit_real = correlation * inverse
+            unit_imag = quadrature * inverse
+            if hour == 0:
+                linear, mean_real, mean_imag = correlation, unit_real, unit_imag
+            else:
+                linear = linear + correlation
+                mean_real = mean_real + unit_real
+                mean_imag = mean_imag + unit_imag
+        stacked = linear * (mean_real * mean_real + mean_imag * mean_imag) * (1.0 / HOURS**3)
+        live = step * out.shape[0] + slot < live_ref[0]
+        out[slot] = jnp.where(live, stacked, jnp.zeros_like(stacked))
 
 
 def on_device(spectra, pair_blocks, block_count):
@@ -179,12 +179,12 @@
     spectra = spectra[:, 0]
     wide = spectra.astype(jnp.float32)
     magnitude = magnitude_of(wide[0], wide[1]).astype(jnp.bfloat16)
-    twin = lax.ppermute(spectra, "pairs", [(i, i ^ 1) for i in range(OWNERS)])
+    twins = [(i, i ^ 1) for i in range(OWNERS)]
+    twin = lax.ppermute(spectra, "pairs", twins)
     last = OWNERS - 1
     near_pairs = [(i, i + 1) for i in range(1, last, 2)] + [(i, i - 1) for i in range(2, last, 2)]
-    far_pairs = [(i, i + 2) for i in range(1, last - 1, 2)] + [(i, i - 2) for i in range(2, last, 2)]
     near = lax.ppermute(magnitude, "pairs", near_pairs)
-    far = lax.ppermute(magnitude, "pairs", far_pairs)
+    far = lax.ppermute(near, "pairs", twins)
     vmem = pl.BlockSpec(memory_space=pltpu.VMEM)
     smem = pl.BlockSpec(memory_space=pltpu.SMEM)
     packed = pl.pallas_call(
@@ -221,7 +221,7 @@
         out_shape=jax.ShapeDtypeStruct((MAXB, CB, LAG_PART), jnp.float32),
         in_specs=[
             smem,
-            pl.BlockSpec((2 * LAG_PART, 2 * ROWS_PART), lambda i: (0, 0)),
+            pl.BlockSpec((2 * ROWS_PART, 2 * LAG_PART), lambda i: (0, 0)),
             pl.BlockSpec((HOURS, ROWS_PART, slots * CB), lambda i: (0, 0, i)),
         ],
         out_specs=pl.BlockSpec((slots, CB, LAG_PART), lambda i: (i, 0, 0)),

time: 80.1 us -> 75.2 us (0.939)
  Pallas kernels: 12.5 us -> 9.32 us
  starting transfers between devices: 14.7 us -> 12.9 us
    ppermute x2, starting transfers between devices: 4.15 us -> 0.21 us  [the longest x1 0.12 us: on_device(): far = lax.ppermute(near, 'pairs', twins)]
    pallas_call x1, Pallas kernels: 6.27 us -> 3.25 us  [on_device(): pl.pallas_call(cross_kernel, out_shape=jax.ShapeDtypeStruct((CHIPS, ROWS_...]
    ppermute x1, starting transfers between devices: 1.92 us -> 4.09 us  [on_device(): near = lax.ppermute(magnitude, 'pairs', near_pairs)]
    ppermute x2, waiting for transfers between devices: 1.98 us -> 1.14 us  [the longest x1 1.13 us: on_device(): far = lax.ppermute(near, 'pairs', twins)]
where the time goes in v2:
time: 75.2 us; the launch traced here: 74.8 us
  waiting for transfers between devices  27 us (36%)
  blocking collectives  23.2 us (31%)
  starting transfers between devices  12.9 us (17%)
  Pallas kernels  9.32 us (12%)
  other arithmetic  1.38 us (2%)
  local copies, waits for them, and re-layouts  0.86 us (1%)
    all_to_all x1, blocking collectives, on_device(): lax.all_to_all(packed, 'pairs', 0, 0, axis_index_groups=groups, tiled=True)  23.2 us
    all_to_all x1, waiting for transfers between devices, on_device(): parts = lax.all_to_all(parts, 'tm', 0, 0, tiled=True)  21.8 us
    all_to_all x1, starting transfers between devices, on_device(): parts = lax.all_to_all(parts, 'tm', 0, 0, tiled=True)  8.6 us
    ppermute x1, starting transfers between devices, on_device(): near = lax.ppermute(magnitude, 'pairs', near_pairs)  4.09 us
    ppermute x1, waiting for transfers between devices, on_device(): near = lax.ppermute(magnitude, 'pairs', near_pairs)  4.04 us
    pallas_call x1, Pallas kernels, on_device(): pl.pallas_call(stack_kernel, grid=(MAXB // slots,), out_shape=jax.ShapeDt...  3.4 us
    pallas_call x1, Pallas kernels, on_device(): pl.pallas_call(cross_kernel, out_shape=jax.ShapeDtypeStruct((CHIPS, ROWS_...  3.25 us
    pallas_call x1, Pallas kernels, on_device(): pl.pallas_call(combine_kernel, out_shape=jax.ShapeDtypeStruct((HOURS * RO...  2.67 us
  transfers between devices with their start and end apart: 4, of which 3 were waited for; matrix products, arithmetic and copies ran while one was open for 3% of the time, Pallas kernels for 0%

profile of v2, /device:TPU:8, one launch (start us, length us, event | category | flops | bytes accessed | tf_op | source)
XLA Modules:
  0.0 74.8 jit_solution(16013582982284820259)
XLA Ops:
  0.0 0.0 copy-start.5
  0.0 0.1 collective-permute-start
  0.1 1.2 %bitcast_convert_fusion = f32[2,32,4096]{2,1,0:T(8,128)S(1)} fusion(bf16[2,1,32,4096]{3,2,1,0:T(8,128)(2,1)} %param.8), kind=kLoop, calls=%fused_computation.6 | loop fusion | flops 262144 | bytes 1572864 | tf_op jit(solution)/shard_map/convert_element_type | solution.py:180
  1.3 0.2 fusion.3
  1.5 4.1 %collective-permute-start.1 = (bf16[32,4096]{1,0:T(8,128)(2,1)S(1)}, bf16[32,4096]{1,0:T(8,128)(2,1)S(1)}, u32[]{:S(2)}, u32[]{:S(2)}) collective-permute-start(bf16[32,4096]{1,0:T(8,128)(2,1)S(1)} %fusion.3), channel_id=1, source_target_pairs={{8,16},{24,32},{40,48},{56,64},{72,80},{88,96},{104,112},{120,128}... | collective-permute-start | bytes 786440 | tf_op jit(solution)/shard_map/ppermute | solution.py:186
  5.6 4.0 %collective-permute-done.1.near = bf16[32,4096]{1,0:T(8,128)(2,1)S(1)} collective-permute-done((bf16[32,4096]{1,0:T(8,128)(2,1)S(1)}, bf16[32,4096]{1,0:T(8,128)(2,1)S(1)}, u32[]{:S(2)}, u32[]{:S(2)}) %collective-permute-start.1) | collective-permute-done | bytes 262176 | tf_op jit(solution)/shard_map/ppermute | solution.py:186
  9.7 0.1 collective-permute-start.2
  9.8 0.0 copy-done.6
  9.8 0.1 copy.9
  9.9 0.1 reshape.14.blocks
  10.0 0.0 collective-permute-done.twin
  10.1 1.1 %collective-permute-done.2.far = bf16[32,4096]{1,0:T(8,128)(2,1)S(1)} collective-permute-done((bf16[32,4096]{1,0:T(8,128)(2,1)S(1)}, bf16[32,4096]{1,0:T(8,128)(2,1)S(1)}, u32[]{:S(2)}, u32[]{:S(2)}) %collective-permute-start.2) | collective-permute-done | bytes 262176 | tf_op jit(solution)/shard_map/ppermute | solution.py:187
  11.2 0.0 copy-done
  11.2 0.0 copy-done.4
  11.2 0.0 copy-done.5
  11.2 0.0 copy-start.2
  11.2 3.3 %cross.1 = bf16[16,56,512]{2,1,0:T(8,128)(2,1)S(1)} custom-call(s32[256]{0:T(256)S(1)} %reshape.14.blocks, s32[1]{0:T(128)} %bitcast.core_ref, bf16[2,32,4096]{2,1,0:T(8,128)(2,1)S(1)} %bitcast.9, bf16[2,32,4096]{2,1,0:T(8,128)(2,1)S(1)} %collective-permute-done.twin, bf16[32,4096]{1,0:T(8,128)(2,1)S(1)} %collective-permute-done.1.near, ...), custom_call_target="tpu_custom_call" | custom-call | tf_op jit(solution)/shard_map/cross/pallas_call | solution.py:190
  14.5 0.0 copy-start.1
  14.5 23.2 %all_to_all.10 = bf16[16,56,512]{2,1,0:T(8,128)(2,1)S(1)} all-to-all(bf16[16,56,512]{2,1,0:T(8,128)(2,1)S(1)} %cross.1), channel_id=1, replica_groups={{0,16,32,48,64,80,96,112,128,144,160,176,192,208,224,240},{8,24,40,56,7..., dimensions={0} | all-to-all | bytes 1835008 | tf_op jit(solution)/shard_map/all_to_all | solution.py:204
  37.7 2.7 %combine.1 = bf16[768,512]{1,0:T(8,128)(2,1)} custom-call(bf16[768,896]{1,0:T(8,128)(2,1)S(1)} %copy-done.2, bf16[768,896]{1,0:T(8,128)(2,1)S(1)} %copy-done.1, bf16[896,512]{1,0:T(8,128)(2,1)S(1)} %bitcast.7), custom_call_target="tpu_custom_call" | custom-call | tf_op jit(solution)/shard_map/combine/pallas_call | solution.py:206
  40.4 8.6 %all-to-all-start.1 = ((bf16[8,96,512]{2,1,0:T(8,128)(2,1)}), bf16[8,96,512]{2,1,0:T(8,128)(2,1)S(1)}, u32[]{:S(2)}, u32[]{:S(2)}) async-start(bf16[8,96,512]{2,1,0:T(8,128)(2,1)} %bitcast.4), calls=%async_computation.1 | async-start | bytes 1572864 | tf_op jit(solution)/shard_map/all_to_all | solution.py:215
  49.0 0.6 dynamic_slice.4.live_ref
  49.6 21.8 %all-to-all-done.1.parts = bf16[8,96,512]{2,1,0:T(8,128)(2,1)S(1)} async-done(((bf16[8,96,512]{2,1,0:T(8,128)(2,1)}), bf16[8,96,512]{2,1,0:T(8,128)(2,1)S(1)}, u32[]{:S(2)}, u32[]{:S(2)}) %all-to-all-start.1) | async-done | bytes 786464 | tf_op jit(solution)/shard_map/all_to_all | solution.py:215
  71.4 3.4 %stack.1 = f32[4,128,256]{2,1,0:T(8,128)} custom-call(s32[1]{0:T(128)} %dynamic_slice.4.live_ref, bf16[192,512]{1,0:T(8,128)(2,1)S(1)} %copy-done.3, bf16[8,96,512]{2,1,0:T(8,128)(2,1)S(1)} %all-to-all-done.1.parts), custom_call_target="tpu_custom_call" | custom-call | tf_op jit(solution)/shard_map/stack/pallas_call | solution.py:218
  (9 shorter events, 0.0 us)
Async XLA Ops:
  0.0 9.8 %copy-start.6 = (s32[32,4,2]{0,2,1:T(2,128)S(1)}, s32[32,4,2]{0,2,1:T(2,128)}, u32[]{:S(2)}) copy-start(s32[32,4,2]{0,2,1:T(2,128)} %param.9) | copy-start | bytes 3076
  0.0 11.2 %copy-start = (bf16[2,1,32,4096]{3,2,1,0:T(8,128)(2,1)S(1)}, bf16[2,1,32,4096]{3,2,1,0:T(8,128)(2,1)}, u32[]{:S(2)}) copy-start(bf16[2,1,32,4096]{3,2,1,0:T(8,128)(2,1)} %param.8) | copy-start | bytes 1572868
  0.0 11.2 %copy-start.4 = (bf16[56,256]{1,0:T(8,128)(2,1)S(1)}, bf16[56,256]{1,0:T(8,128)(2,1)}, u32[]{:S(2)}) copy-start(bf16[56,256]{1,0:T(8,128)(2,1)} %constant.35.clone.compress) | copy-start | bytes 86020
  0.0 11.2 %copy-start.5 = (bf16[64,128]{1,0:T(8,128)(2,1)S(1)}, bf16[64,128]{1,0:T(8,128)(2,1)}, u32[]{:S(2)}) copy-start(bf16[64,128]{1,0:T(8,128)(2,1)} %constant.34.clone.window) | copy-start | bytes 49156
  0.0 10.0 %collective-permute-start = (bf16[2,32,4096]{2,1,0:T(8,128)(2,1)}, bf16[2,32,4096]{2,1,0:T(8,128)(2,1)S(1)}, u32[]{:S(2)}, u32[]{:S(2)}) collective-permute-start(bf16[2,32,4096]{2,1,0:T(8,128)(2,1)} %bitcast.8), channel_id=1, source_target_pairs={{0,8},{8,0},{16,24},{24,16},{32,40},{40,32},{48,56},{56,48},{64,72... | collective-permute-start | bytes 1572872 | tf_op jit(solution)/shard_map/ppermute | solution.py:183
  1.5 8.1 %collective-permute-start.1 = (bf16[32,4096]{1,0:T(8,128)(2,1)S(1)}, bf16[32,4096]{1,0:T(8,128)(2,1)S(1)}, u32[]{:S(2)}, u32[]{:S(2)}) collective-permute-start(bf16[32,4096]{1,0:T(8,128)(2,1)S(1)} %fusion.3), channel_id=1, source_target_pairs={{8,16},{24,32},{40,48},{56,64},{72,80},{88,96},{104,112},{120,128}... | collective-permute-start | bytes 786440 | tf_op jit(solution)/shard_map/ppermute | solution.py:186
  9.7 1.5 %collective-permute-start.2 = (bf16[32,4096]{1,0:T(8,128)(2,1)S(1)}, bf16[32,4096]{1,0:T(8,128)(2,1)S(1)}, u32[]{:S(2)}, u32[]{:S(2)}) collective-permute-start(bf16[32,4096]{1,0:T(8,128)(2,1)S(1)} %collective-permute-done.1.near), channel_id=1, source_target_pairs={{0,8},{8,0},{16,24},{24,16},{32,40},{40,32},{48,56},{56,48},{64,72... | collective-permute-start | bytes 786440 | tf_op jit(solution)/shard_map/ppermute | solution.py:187
  11.2 26.5 %copy-start.2 = (bf16[768,896]{1,0:T(8,128)(2,1)S(1)}, bf16[768,896]{1,0:T(8,128)(2,1)}, u32[]{:S(2)}) copy-start(bf16[768,896]{1,0:T(8,128)(2,1)} %constant.36.clone.high) | copy-start | bytes 4128772
  14.5 23.2 %copy-start.1 = (bf16[768,896]{1,0:T(8,128)(2,1)S(1)}, bf16[768,896]{1,0:T(8,128)(2,1)}, u32[]{:S(2)}) copy-start(bf16[768,896]{1,0:T(8,128)(2,1)} %constant.37.clone.low) | copy-start | bytes 4128772
  40.4 8.6 %copy-start.7 = (s32[32]{0:T(128)S(1)}, s32[32]{0:T(128)}, u32[]{:S(2)}) copy-start(s32[32]{0:T(128)} %param.10) | copy-start | bytes 388
  40.4 31.0 %copy-start.3 = (bf16[192,512]{1,0:T(8,128)(2,1)S(1)}, bf16[192,512]{1,0:T(8,128)(2,1)}, u32[]{:S(2)}) copy-start(bf16[192,512]{1,0:T(8,128)(2,1)} %constant.38.clone.expand) | copy-start | bytes 589828
  40.4 31.0 %all-to-all-start.1 = ((bf16[8,96,512]{2,1,0:T(8,128)(2,1)}), bf16[8,96,512]{2,1,0:T(8,128)(2,1)S(1)}, u32[]{:S(2)}, u32[]{:S(2)}) async-start(bf16[8,96,512]{2,1,0:T(8,128)(2,1)} %bitcast.4), calls=%async_computation.1 | async-start | bytes 1572864 | tf_op jit(solution)/shard_map/all_to_all | solution.py:215

commit v3 on v2

v3 whole, which is shorter than its diff:
```python
import functools
import math

import jax
import jax.numpy as jnp
import ml_dtypes
import numpy as np
from jax import lax
from jax.experimental import pallas as pl
from jax.experimental.pallas import tpu as pltpu
from jax.sharding import PartitionSpec as P

C = 4096
CB = 128
NF = 1024
FIRST_BIN = 16
FFT_LEN = 8192
LAGS = 2048
SMOOTH = 32
MAXB = 4
HOURS = 8
OWNERS = 32
amp_floor = 0.2

CHIPS = OWNERS // 2
BINS = NF // OWNERS
CHIP_BINS = 2 * BINS
LAG_PART = LAGS // HOURS
RANK_CHIP = 28
RANK_PART = 48
ROWS_CHIP = 2 * RANK_CHIP
ROWS_PART = 2 * RANK_PART
STEP = 2.0 * math.pi / FFT_LEN


def slepian(points, half_width, count):
    n = np.arange(points, dtype=np.float64)
    tri = np.diag(((points - 1) / 2.0 - n) ** 2 * math.cos(2.0 * math.pi * half_width))
    off = n[1:] * (points - n[1:]) / 2.0
    tri = tri + np.diag(off, 1) + np.diag(off, -1)
    vectors = np.linalg.eigh(tri)[1][:, ::-1][:, :count]
    return vectors * np.where(vectors[points // 2] < 0, -1.0, 1.0)


def split_rounded(table):
    high = table.astype(ml_dtypes.bfloat16)
    low = (table - high.astype(np.float64)).astype(ml_dtypes.bfloat16)
    return high, low


def real_form(table):
    return np.block([[table.real, -table.imag], [table.imag, table.real]])


@functools.cache
def tables():
    chip_basis = slepian(CHIP_BINS, LAGS / 2 / FFT_LEN, RANK_CHIP)
    part_basis = slepian(NF, LAG_PART / 2 / FFT_LEN, RANK_PART)
    bins = np.arange(NF) - (NF - 1) / 2.0
    lags = np.arange(LAG_PART) - LAG_PART // 2
    mid_bin = FIRST_BIN + (NF - 1) / 2.0
    compress = np.kron(np.eye(2), chip_basis.T)
    parts = []
    for part in range(HOURS // 2):
        mid_lag = LAG_PART * part - (LAGS - LAG_PART) // 2
        turned = np.exp(1j * STEP * (bins + mid_bin) * mid_lag)[:, None] * part_basis
        turned = turned.reshape(CHIPS, CHIP_BINS, RANK_PART)
        blocks = [(chip_basis.T @ turned[chip]).T for chip in range(CHIPS)]
        parts.append(np.concatenate(blocks, axis=1))
    combine = np.concatenate(parts, axis=0)
    combine = np.concatenate([combine.real, combine.imag], axis=0)
    waves = np.exp(1j * STEP * np.outer(lags, bins)) @ part_basis
    waves = waves * np.exp(1j * STEP * mid_bin * lags)[:, None] / math.sqrt(NF)
    expand = real_form(waves)
    row = np.arange(BINS)[:, None] + SMOOTH
    column = np.arange(BINS + 2 * SMOOTH)[None, :]
    window = (np.abs(row - column) <= SMOOTH).astype(ml_dtypes.bfloat16)
    turned = [window[:, -SMOOTH:], window[:, SMOOTH:-SMOOTH], window[:, :SMOOTH]]
    window = np.stack([window, np.concatenate(turned, axis=1)])
    halves = np.split(compress, 2 * CHIP_BINS // BINS, axis=1)
    by_core = []
    for core in range(2):
        own, twin = core, 1 - core
        ordered = [halves[own], halves[2 + own], halves[twin], halves[2 + twin]]
        by_core.append(np.concatenate(split_rounded(np.concatenate(ordered, axis=1)), axis=1))
    compress = np.stack(by_core)
    expand = np.ascontiguousarray(np.concatenate(split_rounded(expand), axis=1).T)
    return window, compress, split_rounded(combine), expand


def magnitude_of(real, imag):
    real, imag = real.astype(jnp.float32), imag.astype(jnp.float32)
    return jnp.sqrt(real * real + imag * imag).astype(jnp.bfloat16)


def whiten(core, window, source, first, centre, second, white):
    chunk = 512
    weights = window[core]
    for start in range(0, C, chunk):
        lanes = slice(start, start + chunk)
        sizes = jnp.concatenate([first[:, lanes], centre[:, lanes], second[:, lanes]], axis=0)
        sums = jnp.dot(weights, sizes, preferred_element_type=jnp.float32)
        inverse = 1.0 / (sums * (1.0 / (2 * SMOOTH + 1)) + 1e-05)
        for part in range(2):
            value = source[part, :, lanes].astype(jnp.float32) * inverse
            white[part, :, lanes] = value.astype(jnp.bfloat16)


def cross_of(blocks, base, white):
    crossed = []
    for slot in range(MAXB):
        left = pl.ds(pl.multiple_of(blocks[base + 2 * slot] * CB, CB), CB)
        right = pl.ds(pl.multiple_of(blocks[base + 2 * slot + 1] * CB, CB), CB)
        left_re = white[0, :, left].astype(jnp.float32)
        left_im = white[1, :, left].astype(jnp.float32)
        right_re = white[0, :, right].astype(jnp.float32)
        right_im = white[1, :, right].astype(jnp.float32)
        real = left_re * right_re + left_im * right_im
        imag = left_im * right_re - left_re * right_im
        crossed.append(jnp.concatenate([real, imag], axis=0).astype(jnp.bfloat16))
    return jnp.concatenate(crossed, axis=1)


def own_kernel(blocks, core_ref, window, own, near, own_size, twin_size, out, white):
    core = core_ref[0]
    whiten(core, window, own, near, own_size, twin_size, white)
    for chip in range(CHIPS):
        out[chip] = cross_of(blocks, (2 * chip + core) * (2 * MAXB), white)


def twin_kernel(
    blocks, core_ref, window, compress, twin, own_size, twin_size, far, own_cross, out, white
):
    core = core_ref[0]
    whiten(core, window, twin, own_size, twin_size, far, white)
    weights = compress[core]
    for chip in range(CHIPS):
        twin_cross = cross_of(blocks, (2 * chip + core) * (2 * MAXB), white)
        cross = jnp.concatenate([own_cross[chip], twin_cross] * 2, axis=0)
        packed = jnp.dot(weights, cross, preferred_element_type=jnp.float32)
        out[chip] = packed.astype(jnp.bfloat16)


def combine_kernel(high, low, packed, out):
    real = jnp.concatenate([packed[chip, :RANK_CHIP] for chip in range(CHIPS)], axis=0)
    imag = jnp.concatenate([packed[chip, RANK_CHIP:] for chip in range(CHIPS)], axis=0)
    value = jnp.concatenate([real, imag], axis=1)
    total = jnp.dot(high[...], value, preferred_element_type=jnp.float32)
    total = total + jnp.dot(low[...], value, preferred_element_type=jnp.float32)
    half = HOURS // 2 * RANK_PART
    wide = MAXB * CB
    for part in range(HOURS // 2):
        rows = slice(part * RANK_PART, (part + 1) * RANK_PART)
        turned = slice(half + part * RANK_PART, half + (part + 1) * RANK_PART)
        real_real, real_imag = total[rows, :wide], total[rows, wide:]
        imag_real, imag_imag = total[turned, :wide], total[turned, wide:]
        for where, sign in ((part, 1.0), (HOURS - 1 - part, -1.0)):
            out[where, :RANK_PART] = (real_real - sign * imag_imag).astype(jnp.bfloat16)
            out[where, RANK_PART:] = (real_imag + sign * imag_real).astype(jnp.bfloat16)


def stack_kernel(live_ref, expand, parts, out):
    step = pl.program_id(0)
    for slot in range(out.shape[0]):
        lanes = slice(slot * CB, (slot + 1) * CB)
        linear = mean_real = mean_imag = None
        for hour in range(HOURS):
            part = parts[hour, :, lanes]
            part = jnp.concatenate([part, part], axis=0)
            lagged = lax.dot_general(
                part, expand[...], (((0,), (0,)), ((), ())), preferred_element_type=jnp.float32
            )
            correlation = lagged[:, :LAG_PART]
            quadrature = lagged[:, LAG_PART:]
            power = correlation * correlation + quadrature * quadrature
            inverse = jnp.minimum(lax.rsqrt(power), 1.0 / amp_floor)
            unit_real = correlation * inverse
            unit_imag = quadrature * inverse
            if hour == 0:
                linear, mean_real, mean_imag = correlation, unit_real, unit_imag
            else:
                linear = linear + correlation
                mean_real = mean_real + unit_real
                mean_imag = mean_imag + unit_imag
        stacked = linear * (mean_real * mean_real + mean_imag * mean_imag) * (1.0 / HOURS**3)
        live = step * out.shape[0] + slot < live_ref[0]
        out[slot] = jnp.where(live, stacked, jnp.zeros_like(stacked))


def on_device(spectra, pair_blocks, block_count):
    owner = lax.axis_index("pairs")
    core = owner % 2
    window, compress, (high, low), expand = tables()
    spectra = spectra[:, 0]
    twins = [(i, i ^ 1) for i in range(OWNERS)]
    twin = lax.ppermute(spectra, "pairs", twins)
    own_size = magnitude_of(spectra[0], spectra[1])
    last = OWNERS - 1
    near_pairs = [(i, i + 1) for i in range(1, last, 2)] + [(i, i - 1) for i in range(2, last, 2)]
    near = lax.ppermute(own_size, "pairs", near_pairs)
    far = lax.ppermute(near, "pairs", twins)
    twin_size = magnitude_of(twin[0], twin[1])
    vmem = pl.BlockSpec(memory_space=pltpu.VMEM)
    smem = pl.BlockSpec(memory_space=pltpu.SMEM)
    limit = pltpu.CompilerParams(vmem_limit_bytes=32 * 2**20)
    slots = pair_blocks.reshape(-1)
    white = pltpu.VMEM((2, BINS, C), jnp.bfloat16)
    own_cross = pl.pallas_call(
        own_kernel,
        out_shape=jax.ShapeDtypeStruct((CHIPS, 2 * BINS, MAXB * CB), jnp.bfloat16),
        in_specs=[smem, smem] + [vmem] * 5,
        out_specs=vmem,
        scratch_shapes=[white],
        compiler_params=limit,
        name="own_cross",
    )(slots, core[None], window, spectra, near, own_size, twin_size)
    packed = pl.pallas_call(
        twin_kernel,
        out_shape=jax.ShapeDtypeStruct((CHIPS, ROWS_CHIP, MAXB * CB), jnp.bfloat16),
        in_specs=[smem, smem] + [vmem] * 7,
        out_specs=vmem,
        scratch_shapes=[white],
        compiler_params=limit,
        name="twin_cross",
    )(slots, core[None], window, compress, twin, own_size, twin_size, far, own_cross)
    groups = [list(range(0, OWNERS, 2)), list(range(1, OWNERS, 2))]
    packed = lax.all_to_all(packed, "pairs", 0, 0, axis_index_groups=groups, tiled=True)
    parts = pl.pallas_call(
        combine_kernel,
        out_shape=jax.ShapeDtypeStruct((HOURS, ROWS_PART, MAXB * CB), jnp.bfloat16),
        in_specs=[vmem] * 3,
        out_specs=vmem,
        compiler_params=pltpu.CompilerParams(vmem_limit_bytes=32 * 2**20),
        name="combine",
    )(high, low, packed)
    parts = lax.all_to_all(parts, "tm", 0, 0, tiled=True)
    live = lax.dynamic_index_in_dim(block_count, owner, 0, keepdims=True)
    slots = 2
    return pl.pallas_call(
        stack_kernel,
        grid=(MAXB // slots,),
        out_shape=jax.ShapeDtypeStruct((MAXB, CB, LAG_PART), jnp.float32),
        in_specs=[
            smem,
            pl.BlockSpec((2 * ROWS_PART, 2 * LAG_PART), lambda i: (0, 0)),
            pl.BlockSpec((HOURS, ROWS_PART, slots * CB), lambda i: (0, 0, i)),
        ],
        out_specs=pl.BlockSpec((slots, CB, LAG_PART), lambda i: (i, 0, 0)),
        compiler_params=pltpu.CompilerParams(vmem_limit_bytes=32 * 2**20),
        name="stack",
    )(live, expand, parts)


def solution(mesh):
    return jax.shard_map(
        on_device,
        mesh=mesh,
        in_specs=(P(None, "tm", "pairs", None), P(), P()),
        out_specs=P("pairs", None, "tm"),
        check_vma=False,
    )
```

time: 75.2 us -> 72.5 us (0.964)
  waiting for transfers between devices: 27 us -> 24.2 us
    sqrt x0 -> x2, other arithmetic: none -> 1.47 us  [magnitude_of(): return jnp.sqrt(real * real + imag * imag).astype(jnp.bfloat16)]
    all_to_all x1, waiting for transfers between devices: 21.8 us -> 20.4 us  [on_device(): parts = lax.all_to_all(parts, 'tm', 0, 0, tiled=True)]
    convert_element_type x2 -> x0, other arithmetic: 1.38 us -> none  [the longest x1 1.19 us: on_device(): wide = spectra.astype(jnp.float32)]
    ppermute x1, waiting for transfers between devices: 1.13 us -> 0.01 us  [on_device(): far = lax.ppermute(near, 'pairs', twins)]
    pallas_call x2 -> x3, Pallas kernels: 5.92 us -> 5.23 us  [the longest x1 1.93 us: on_device(): pl.pallas_call(twin_kernel, out_shape=jax.ShapeDtypeStruct((CHIPS, ROWS_C...]
  transfers between devices with their start and end apart: 4 -> 4, of which waited for: 3 -> 2; matrix products, arithmetic and copies ran while one was open for 3% -> 3% of each run, Pallas kernels for 0% -> 2%
where the time goes in v3:
time: 72.5 us; the launch traced here: 72 us
  waiting for transfers between devices  24.2 us (33%)
  blocking collectives  23 us (32%)
  starting transfers between devices  13.1 us (18%)
  Pallas kernels  8.63 us (12%)
  local copies, waits for them, and re-layouts  1.51 us (2%)
  other arithmetic  1.47 us (2%)
    all_to_all x1, blocking collectives, on_device(): lax.all_to_all(packed, 'pairs', 0, 0, axis_index_groups=groups, tiled=True)  23 us
    all_to_all x1, waiting for transfers between devices, on_device(): parts = lax.all_to_all(parts, 'tm', 0, 0, tiled=True)  20.4 us
    all_to_all x1, starting transfers between devices, on_device(): parts = lax.all_to_all(parts, 'tm', 0, 0, tiled=True)  8.59 us
    ppermute x1, starting transfers between devices, on_device(): near = lax.ppermute(own_size, 'pairs', near_pairs)  4.34 us
    ppermute x1, waiting for transfers between devices, on_device(): near = lax.ppermute(own_size, 'pairs', near_pairs)  3.73 us
    pallas_call x1, Pallas kernels, on_device(): pl.pallas_call(stack_kernel, grid=(MAXB // slots,), out_shape=jax.ShapeDt...  3.4 us
    pallas_call x1, Pallas kernels, on_device(): pl.pallas_call(twin_kernel, out_shape=jax.ShapeDtypeStruct((CHIPS, ROWS_C...  1.93 us
    pallas_call x1, Pallas kernels, on_device(): pl.pallas_call(combine_kernel, out_shape=jax.ShapeDtypeStruct((HOURS, ROW...  1.87 us
  transfers between devices with their start and end apart: 4, of which 2 were waited for; matrix products, arithmetic and copies ran while one was open for 3% of the time, Pallas kernels for 2%

profile of v3, /device:TPU:8, one launch (start us, length us, event | category | flops | bytes accessed | tf_op | source)
XLA Modules:
  0.0 72.0 jit_solution(7840954952346797893)
XLA Ops:
  0.0 0.0 collective-permute-start
  0.0 1.3 %fusion.own_size = bf16[32,4096]{1,0:T(8,128)(2,1)S(1)} fusion(bf16[2,1,32,4096]{3,2,1,0:T(8,128)(2,1)} %param.8), kind=kLoop, calls=%fused_computation.2 | loop fusion | flops 786432 | bytes 786432 | tf_op jit(solution)/shard_map/sqrt | solution.py:93
  1.3 0.0 copy-start
  1.3 4.3 %collective-permute-start.1 = (bf16[32,4096]{1,0:T(8,128)(2,1)S(1)}, bf16[32,4096]{1,0:T(8,128)(2,1)S(1)}, u32[]{:S(2)}, u32[]{:S(2)}) collective-permute-start(bf16[32,4096]{1,0:T(8,128)(2,1)S(1)} %fusion.own_size), channel_id=1, source_target_pairs={{8,16},{24,32},{40,48},{56,64},{72,80},{88,96},{104,112},{120,128}... | collective-permute-start | bytes 786440 | tf_op jit(solution)/shard_map/ppermute | solution.py:200
  5.6 0.1 copy.9
  5.8 0.1 reshape.21.blocks
  5.9 0.0 copy-start.4
  5.9 3.7 %collective-permute-done.1.near = bf16[32,4096]{1,0:T(8,128)(2,1)S(1)} collective-permute-done((bf16[32,4096]{1,0:T(8,128)(2,1)S(1)}, bf16[32,4096]{1,0:T(8,128)(2,1)S(1)}, u32[]{:S(2)}, u32[]{:S(2)}) %collective-permute-start.1) | collective-permute-done | bytes 262176 | tf_op jit(solution)/shard_map/ppermute | solution.py:200
  9.7 0.1 collective-permute-start.2
  9.8 0.0 collective-permute-done.twin
  9.8 0.2 fusion.1.twin_size
  10.0 0.0 copy-start.5
  10.0 1.4 %own_cross.1 = bf16[16,64,512]{2,1,0:T(8,128)(2,1)S(1)} custom-call(s32[256]{0:T(256)S(1)} %reshape.21.blocks, s32[1]{0:T(128)} %bitcast.core_ref, bf16[2,32,96]{2,1,0:T(8,128)(2,1)S(1)} %copy-done.4, bf16[2,32,4096]{2,1,0:T(8,128)(2,1)S(1)} %bitcast.7, bf16[32,4096]{1,0:T(8,128)(2,1)S(1)} %collective-permute-done.1.near, ...), custom_call_target="tpu_custom_call" | custom-call | tf_op jit(solution)/shard_map/own_cross/pallas_call | solution.py:208
  11.5 0.0 collective-permute-done.2.far
  11.5 1.9 %twin_cross.1 = bf16[16,56,512]{2,1,0:T(8,128)(2,1)S(1)} custom-call(s32[256]{0:T(256)S(1)} %reshape.21.blocks, s32[1]{0:T(128)} %bitcast.core_ref, bf16[2,32,96]{2,1,0:T(8,128)(2,1)S(1)} %copy-done.4, bf16[2,56,256]{2,1,0:T(8,128)(2,1)S(1)} %copy-done.5, bf16[2,32,4096]{2,1,0:T(8,128)(2,1)S(1)} %collective-permute-done.twin, ...), custom_call_target="tpu_custom_call" | custom-call | tf_op jit(solution)/shard_map/twin_cross/pallas_call | solution.py:217
  13.4 0.0 copy-start.1
  13.5 0.0 copy-start.2
  13.5 23.0 %all_to_all.10.packed = bf16[16,56,512]{2,1,0:T(8,128)(2,1)S(1)} all-to-all(bf16[16,56,512]{2,1,0:T(8,128)(2,1)S(1)} %twin_cross.1), channel_id=1, replica_groups={{0,16,32,48,64,80,96,112,128,144,160,176,192,208,224,240},{8,24,40,56,7..., dimensions={0} | all-to-all | bytes 1835008 | tf_op jit(solution)/shard_map/all_to_all | solution.py:227
  36.5 1.9 %combine.1 = bf16[8,96,512]{2,1,0:T(8,128)(2,1)} custom-call(bf16[384,448]{1,0:T(8,128)(2,1)S(1)} %copy-done.2, bf16[384,448]{1,0:T(8,128)(2,1)S(1)} %copy-done.1, bf16[16,56,512]{2,1,0:T(8,128)(2,1)S(1)} %all_to_all.10.packed), custom_call_target="tpu_custom_call" | custom-call | tf_op jit(solution)/shard_map/combine/pallas_call | solution.py:228
  38.4 8.6 %all-to-all-start.1 = ((bf16[8,96,512]{2,1,0:T(8,128)(2,1)}), bf16[8,96,512]{2,1,0:T(8,128)(2,1)S(1)}, u32[]{:S(2)}, u32[]{:S(2)}) async-start(bf16[8,96,512]{2,1,0:T(8,128)(2,1)} %combine.1), calls=%async_computation.1 | async-start | bytes 1572864 | tf_op jit(solution)/shard_map/all_to_all | solution.py:236
  47.0 0.7 copy-done.7
  47.6 0.6 dynamic_slice.4.live_ref
  48.2 20.4 %all-to-all-done.1.parts = bf16[8,96,512]{2,1,0:T(8,128)(2,1)S(1)} async-done(((bf16[8,96,512]{2,1,0:T(8,128)(2,1)}), bf16[8,96,512]{2,1,0:T(8,128)(2,1)S(1)}, u32[]{:S(2)}, u32[]{:S(2)}) %all-to-all-start.1) | async-done | bytes 786464 | tf_op jit(solution)/shard_map/all_to_all | solution.py:236
  68.6 3.4 %stack.1 = f32[4,128,256]{2,1,0:T(8,128)} custom-call(s32[1]{0:T(128)} %dynamic_slice.4.live_ref, bf16[192,512]{1,0:T(8,128)(2,1)S(1)} %copy-done.3, bf16[8,96,512]{2,1,0:T(8,128)(2,1)S(1)} %all-to-all-done.1.parts), custom_call_target="tpu_custom_call" | custom-call | tf_op jit(solution)/shard_map/stack/pallas_call | solution.py:239
  (10 shorter events, 0.0 us)
Async XLA Ops:
  0.0 9.8 %collective-permute-start = (bf16[2,32,4096]{2,1,0:T(8,128)(2,1)}, bf16[2,32,4096]{2,1,0:T(8,128)(2,1)S(1)}, u32[]{:S(2)}, u32[]{:S(2)}) collective-permute-start(bf16[2,32,4096]{2,1,0:T(8,128)(2,1)} %bitcast.6), channel_id=1, source_target_pairs={{0,8},{8,0},{16,24},{24,16},{32,40},{40,32},{48,56},{56,48},{64,72... | collective-permute-start | bytes 1572872 | tf_op jit(solution)/shard_map/ppermute | solution.py:196
  0.0 5.6 %copy-start.6 = (s32[32,4,2]{0,2,1:T(2,128)S(1)}, s32[32,4,2]{0,2,1:T(2,128)}, u32[]{:S(2)}) copy-start(s32[32,4,2]{0,2,1:T(2,128)} %param.9) | copy-start | bytes 3076
  1.3 8.7 %copy-start = (bf16[2,1,32,4096]{3,2,1,0:T(8,128)(2,1)S(1)}, bf16[2,1,32,4096]{3,2,1,0:T(8,128)(2,1)}, u32[]{:S(2)}) copy-start(bf16[2,1,32,4096]{3,2,1,0:T(8,128)(2,1)} %param.8) | copy-start | bytes 1572868
  1.3 8.4 %collective-permute-start.1 = (bf16[32,4096]{1,0:T(8,128)(2,1)S(1)}, bf16[32,4096]{1,0:T(8,128)(2,1)S(1)}, u32[]{:S(2)}, u32[]{:S(2)}) collective-permute-start(bf16[32,4096]{1,0:T(8,128)(2,1)S(1)} %fusion.own_size), channel_id=1, source_target_pairs={{8,16},{24,32},{40,48},{56,64},{72,80},{88,96},{104,112},{120,128}... | collective-permute-start | bytes 786440 | tf_op jit(solution)/shard_map/ppermute | solution.py:200
  5.9 4.1 %copy-start.4 = (bf16[2,32,96]{2,1,0:T(8,128)(2,1)S(1)}, bf16[2,32,96]{2,1,0:T(8,128)(2,1)}, u32[]{:S(2)}) copy-start(bf16[2,32,96]{2,1,0:T(8,128)(2,1)} %constant.34.clone.window) | copy-start | bytes 36868
  9.7 1.8 %collective-permute-start.2 = (bf16[32,4096]{1,0:T(8,128)(2,1)S(1)}, bf16[32,4096]{1,0:T(8,128)(2,1)S(1)}, u32[]{:S(2)}, u32[]{:S(2)}) collective-permute-start(bf16[32,4096]{1,0:T(8,128)(2,1)S(1)} %collective-permute-done.1.near), channel_id=1, source_target_pairs={{0,8},{8,0},{16,24},{24,16},{32,40},{40,32},{48,56},{56,48},{64,72... | collective-permute-start | bytes 786440 | tf_op jit(solution)/shard_map/ppermute | solution.py:201
  10.0 1.5 %copy-start.5 = (bf16[2,56,256]{2,1,0:T(8,128)(2,1)S(1)}, bf16[2,56,256]{2,1,0:T(8,128)(2,1)}, u32[]{:S(2)}) copy-start(bf16[2,56,256]{2,1,0:T(8,128)(2,1)} %constant.35.clone.compress) | copy-start | bytes 172036
  13.4 23.1 %copy-start.1 = (bf16[384,448]{1,0:T(8,128)(2,1)S(1)}, bf16[384,448]{1,0:T(8,128)(2,1)}, u32[]{:S(2)}) copy-start(bf16[384,448]{1,0:T(8,128)(2,1)} %constant.37.clone.low) | copy-start | bytes 1032196
  13.5 23.1 %copy-start.2 = (bf16[384,448]{1,0:T(8,128)(2,1)S(1)}, bf16[384,448]{1,0:T(8,128)(2,1)}, u32[]{:S(2)}) copy-start(bf16[384,448]{1,0:T(8,128)(2,1)} %constant.36.clone.high) | copy-start | bytes 1032196
  38.4 30.3 %copy-start.3 = (bf16[192,512]{1,0:T(8,128)(2,1)S(1)}, bf16[192,512]{1,0:T(8,128)(2,1)}, u32[]{:S(2)}) copy-start(bf16[192,512]{1,0:T(8,128)(2,1)} %constant.38.clone.expand) | copy-start | bytes 589828
  38.4 30.3 %all-to-all-start.1 = ((bf16[8,96,512]{2,1,0:T(8,128)(2,1)}), bf16[8,96,512]{2,1,0:T(8,128)(2,1)S(1)}, u32[]{:S(2)}, u32[]{:S(2)}) async-start(bf16[8,96,512]{2,1,0:T(8,128)(2,1)} %combine.1), calls=%async_computation.1 | async-start | bytes 1572864 | tf_op jit(solution)/shard_map/all_to_all | solution.py:236
  47.0 0.7 copy-start.7

commit v4 on v3

--- a/solution.py
+++ b/solution.py
@@ -67,8 +67,7 @@
         turned = turned.reshape(CHIPS, CHIP_BINS, RANK_PART)
         blocks = [(chip_basis.T @ turned[chip]).T for chip in range(CHIPS)]
         parts.append(np.concatenate(blocks, axis=1))
-    combine = np.concatenate(parts, axis=0)
-    combine = np.concatenate([combine.real, combine.imag], axis=0)
+    combine = np.concatenate([half for part in parts for half in (part.real, part.imag)], axis=0)
     waves = np.exp(1j * STEP * np.outer(lags, bins)) @ part_basis
     waves = waves * np.exp(1j * STEP * mid_bin * lags)[:, None] / math.sqrt(NF)
     expand = real_form(waves)
@@ -84,7 +83,10 @@
         ordered = [halves[own], halves[2 + own], halves[twin], halves[2 + twin]]
         by_core.append(np.concatenate(split_rounded(np.concatenate(ordered, axis=1)), axis=1))
     compress = np.stack(by_core)
-    expand = np.ascontiguousarray(np.concatenate(split_rounded(expand), axis=1).T)
+    padded = np.zeros((2 * CB, 2 * LAG_PART), ml_dtypes.bfloat16)
+    for index, half in enumerate(split_rounded(expand)):
+        padded[index * CB : index * CB + ROWS_PART] = half.T
+    expand = padded
     return window, compress, split_rounded(combine), expand
 
 
@@ -121,57 +123,64 @@
     return jnp.concatenate(crossed, axis=1)
 
 
-def own_kernel(blocks, core_ref, window, own, near, own_size, twin_size, out, white):
-    core = core_ref[0]
+def own_kernel(blocks, window, own, near, own_size, twin_size, out, white):
+    core = blocks[CHIPS * 2 * MAXB]
     whiten(core, window, own, near, own_size, twin_size, white)
     for chip in range(CHIPS):
-        out[chip] = cross_of(blocks, (2 * chip + core) * (2 * MAXB), white)
+        out[chip] = cross_of(blocks, chip * 2 * MAXB, white)
 
 
 def twin_kernel(
-    blocks, core_ref, window, compress, twin, own_size, twin_size, far, own_cross, out, white
+    blocks, window, compress, twin, own_size, twin_size, far, own_cross, out, white
 ):
-    core = core_ref[0]
+    core = blocks[CHIPS * 2 * MAXB]
     whiten(core, window, twin, own_size, twin_size, far, white)
     weights = compress[core]
     for chip in range(CHIPS):
-        twin_cross = cross_of(blocks, (2 * chip + core) * (2 * MAXB), white)
+        twin_cross = cross_of(blocks, chip * 2 * MAXB, white)
         cross = jnp.concatenate([own_cross[chip], twin_cross] * 2, axis=0)
         packed = jnp.dot(weights, cross, preferred_element_type=jnp.float32)
         out[chip] = packed.astype(jnp.bfloat16)
 
 
-def combine_kernel(high, low, packed, out):
+def combine_kernel(high, low, packed, out, parts, sems):
     real = jnp.concatenate([packed[chip, :RANK_CHIP] for chip in range(CHIPS)], axis=0)
     imag = jnp.concatenate([packed[chip, RANK_CHIP:] for chip in range(CHIPS)], axis=0)
     value = jnp.concatenate([real, imag], axis=1)
-    total = jnp.dot(high[...], value, preferred_element_type=jnp.float32)
-    total = total + jnp.dot(low[...], value, preferred_element_type=jnp.float32)
-    half = HOURS // 2 * RANK_PART
     wide = MAXB * CB
+    copies = []
     for part in range(HOURS // 2):
-        rows = slice(part * RANK_PART, (part + 1) * RANK_PART)
-        turned = slice(half + part * RANK_PART, half + (part + 1) * RANK_PART)
-        real_real, real_imag = total[rows, :wide], total[rows, wide:]
-        imag_real, imag_imag = total[turned, :wide], total[turned, wide:]
+        rows = slice(part * ROWS_PART, (part + 1) * ROWS_PART)
+        total = jnp.dot(high[rows], value, preferred_element_type=jnp.float32)
+        total = total + jnp.dot(low[rows], value, preferred_element_type=jnp.float32)
+        real_real, real_imag = total[:RANK_PART, :wide], total[:RANK_PART, wide:]
+        imag_real, imag_imag = total[RANK_PART:, :wide], total[RANK_PART:, wide:]
         for where, sign in ((part, 1.0), (HOURS - 1 - part, -1.0)):
-            out[where, :RANK_PART] = (real_real - sign * imag_imag).astype(jnp.bfloat16)
-            out[where, RANK_PART:] = (real_imag + sign * imag_real).astype(jnp.bfloat16)
-
-
-def stack_kernel(live_ref, expand, parts, out):
-    step = pl.program_id(0)
-    for slot in range(out.shape[0]):
+            both = [real_real - sign * imag_imag, real_imag + sign * imag_real]
+            parts[where] = jnp.concatenate(both, axis=0).astype(jnp.bfloat16)
+            copy = pltpu.make_async_copy(parts.at[where], out.at[where], sems.at[where])
+            copy.start()
+            copies.append(copy)
+    for copy in copies:
+        copy.wait()
+
+
+def stack_kernel(live, expand, parts, out, result, sems):
+    blank = jnp.zeros((CB - ROWS_PART, CB), jnp.bfloat16)
+    copies = []
+    for slot in range(MAXB):
         lanes = slice(slot * CB, (slot + 1) * CB)
+        rows = []
+        for hour in range(HOURS):
+            part = jnp.concatenate([parts[hour, :, lanes], blank], axis=0).T
+            rows.append(jnp.concatenate([part, part], axis=1))
+        lagged = jnp.dot(
+            jnp.concatenate(rows, axis=0), expand[...], preferred_element_type=jnp.float32
+        )
         linear = mean_real = mean_imag = None
         for hour in range(HOURS):
-            part = parts[hour, :, lanes]
-            part = jnp.concatenate([part, part], axis=0)
-            lagged = lax.dot_general(
-                part, expand[...], (((0,), (0,)), ((), ())), preferred_element_type=jnp.float32
-            )
-            correlation = lagged[:, :LAG_PART]
-            quadrature = lagged[:, LAG_PART:]
+            correlation = lagged[hour * CB : (hour + 1) * CB, :LAG_PART]
+            quadrature = lagged[hour * CB : (hour + 1) * CB, LAG_PART:]
             power = correlation * correlation + quadrature * quadrature
             inverse = jnp.minimum(lax.rsqrt(power), 1.0 / amp_floor)
             unit_real = correlation * inverse
@@ -183,8 +192,12 @@
                 mean_real = mean_real + unit_real
                 mean_imag = mean_imag + unit_imag
         stacked = linear * (mean_real * mean_real + mean_imag * mean_imag) * (1.0 / HOURS**3)
-        live = step * out.shape[0] + slot < live_ref[0]
-        out[slot] = jnp.where(live, stacked, jnp.zeros_like(stacked))
+        result[slot] = jnp.where(live[slot] > 0, stacked, jnp.zeros_like(stacked))
+        copy = pltpu.make_async_copy(result.at[slot], out.at[slot], sems.at[slot])
+        copy.start()
+        copies.append(copy)
+    for copy in copies:
+        copy.wait()
 
 
 def on_device(spectra, pair_blocks, block_count):
@@ -203,50 +216,56 @@
     vmem = pl.BlockSpec(memory_space=pltpu.VMEM)
     smem = pl.BlockSpec(memory_space=pltpu.SMEM)
     limit = pltpu.CompilerParams(vmem_limit_bytes=32 * 2**20)
-    slots = pair_blocks.reshape(-1)
+    slots = lax.dynamic_index_in_dim(
+        pair_blocks.reshape(CHIPS, 2, 2 * MAXB), core, 1, keepdims=False
+    )
+    slots = jnp.concatenate([slots.reshape(-1), core[None]])
     white = pltpu.VMEM((2, BINS, C), jnp.bfloat16)
     own_cross = pl.pallas_call(
         own_kernel,
         out_shape=jax.ShapeDtypeStruct((CHIPS, 2 * BINS, MAXB * CB), jnp.bfloat16),
-        in_specs=[smem, smem] + [vmem] * 5,
+        in_specs=[smem] + [vmem] * 5,
         out_specs=vmem,
         scratch_shapes=[white],
         compiler_params=limit,
         name="own_cross",
-    )(slots, core[None], window, spectra, near, own_size, twin_size)
+    )(slots, window, spectra, near, own_size, twin_size)
     packed = pl.pallas_call(
         twin_kernel,
         out_shape=jax.ShapeDtypeStruct((CHIPS, ROWS_CHIP, MAXB * CB), jnp.bfloat16),
-        in_specs=[smem, smem] + [vmem] * 7,
+        in_specs=[smem] + [vmem] * 7,
         out_specs=vmem,
         scratch_shapes=[white],
         compiler_params=limit,
         name="twin_cross",
-    )(slots, core[None], window, compress, twin, own_size, twin_size, far, own_cross)
+    )(slots, window, compress, twin, own_size, twin_size, far, own_cross)
     groups = [list(range(0, OWNERS, 2)), list(range(1, OWNERS, 2))]
     packed = lax.all_to_all(packed, "pairs", 0, 0, axis_index_groups=groups, tiled=True)
     parts = pl.pallas_call(
         combine_kernel,
         out_shape=jax.ShapeDtypeStruct((HOURS, ROWS_PART, MAXB * CB), jnp.bfloat16),
         in_specs=[vmem] * 3,
-        out_specs=vmem,
-        compiler_params=pltpu.CompilerParams(vmem_limit_bytes=32 * 2**20),
+        out_specs=pl.BlockSpec(memory_space=pl.ANY),
+        scratch_shapes=[
+            pltpu.VMEM((HOURS, ROWS_PART, MAXB * CB), jnp.bfloat16),
+            pltpu.SemaphoreType.DMA((HOURS,)),
+        ],
+        compiler_params=limit,
         name="combine",
     )(high, low, packed)
     parts = lax.all_to_all(parts, "tm", 0, 0, tiled=True)
-    live = lax.dynamic_index_in_dim(block_count, owner, 0, keepdims=True)
-    slots = 2
+    count = lax.dynamic_index_in_dim(block_count, owner, 0, keepdims=False)
+    live = (lax.broadcasted_iota(jnp.int32, (MAXB, 1, LAG_PART), 0) < count).astype(jnp.float32)
     return pl.pallas_call(
         stack_kernel,
-        grid=(MAXB // slots,),
         out_shape=jax.ShapeDtypeStruct((MAXB, CB, LAG_PART), jnp.float32),
-        in_specs=[
-            smem,
-            pl.BlockSpec((2 * ROWS_PART, 2 * LAG_PART), lambda i: (0, 0)),
-            pl.BlockSpec((HOURS, ROWS_PART, slots * CB), lambda i: (0, 0, i)),
+        in_specs=[vmem] * 3,
+        out_specs=pl.BlockSpec(memory_space=pl.ANY),
+        scratch_shapes=[
+            pltpu.VMEM((MAXB, CB, LAG_PART), jnp.float32),
+            pltpu.SemaphoreType.DMA((MAXB,)),
         ],
-        out_specs=pl.BlockSpec((slots, CB, LAG_PART), lambda i: (i, 0, 0)),
-        compiler_params=pltpu.CompilerParams(vmem_limit_bytes=32 * 2**20),
+        compiler_params=limit,
         name="stack",
     )(live, expand, parts)
 

time: 72.5 us -> 71.7 us (0.989)
  waiting for transfers between devices: 24.2 us -> 22.6 us
  local copies, waits for them, and re-layouts: 1.51 us -> 2.46 us
  Pallas kernels: 8.63 us -> 7.89 us
    pallas_call x1, Pallas kernels: 3.4 us -> 2.45 us  [on_device(): pl.pallas_call(stack_kernel, out_shape=jax.ShapeDtypeStruct((MAXB, CB, LA...]
    ppermute x1, waiting for transfers between devices: 3.73 us -> 2.86 us  [on_device(): near = lax.ppermute(own_size, 'pairs', near_pairs)]
  transfers between devices with their start and end apart: 4 -> 4, of which waited for: 2 -> 2; matrix products, arithmetic and copies ran while one was open for 3% -> 4% of each run, Pallas kernels for 2% -> 2%
where the time goes in v4:
time: 71.7 us; the launch traced here: 71.3 us
  blocking collectives  23.1 us (32%)
  waiting for transfers between devices  22.6 us (32%)
  starting transfers between devices  12.9 us (18%)
  Pallas kernels  7.89 us (11%)
  local copies, waits for them, and re-layouts  2.46 us (3%)
  other arithmetic  2.12 us (3%)
    all_to_all x1, blocking collectives, on_device(): lax.all_to_all(packed, 'pairs', 0, 0, axis_index_groups=groups, tiled=True)  23.1 us
    all_to_all x1, waiting for transfers between devices, on_device(): parts = lax.all_to_all(parts, 'tm', 0, 0, tiled=True)  19.8 us
    all_to_all x1, starting transfers between devices, on_device(): parts = lax.all_to_all(parts, 'tm', 0, 0, tiled=True)  8.61 us
    ppermute x1, starting transfers between devices, on_device(): near = lax.ppermute(own_size, 'pairs', near_pairs)  4.21 us
    ppermute x1, waiting for transfers between devices, on_device(): near = lax.ppermute(own_size, 'pairs', near_pairs)  2.86 us
    pallas_call x1, Pallas kernels, on_device(): pl.pallas_call(stack_kernel, out_shape=jax.ShapeDtypeStruct((MAXB, CB, LA...  2.45 us
    pallas_call x1, Pallas kernels, on_device(): pl.pallas_call(combine_kernel, out_shape=jax.ShapeDtypeStruct((HOURS, ROW...  2.08 us
    pallas_call x1, Pallas kernels, on_device(): pl.pallas_call(twin_kernel, out_shape=jax.ShapeDtypeStruct((CHIPS, ROWS_C...  1.92 us
  transfers between devices with their start and end apart: 4, of which 2 were waited for; matrix products, arithmetic and copies ran while one was open for 4% of the time, Pallas kernels for 2%

profile of v4, /device:TPU:8, one launch (start us, length us, event | category | flops | bytes accessed | tf_op | source)
XLA Modules:
  0.0 71.3 jit_solution(10422256880588368505)
XLA Ops:
  0.0 1.2 %fusion.own_size = bf16[32,4096]{1,0:T(8,128)(2,1)S(1)} fusion(bf16[2,1,32,4096]{3,2,1,0:T(8,128)(2,1)} %param.8), kind=kLoop, calls=%fused_computation.2 | loop fusion | flops 786432 | bytes 786432 | tf_op jit(solution)/shard_map/sqrt | solution.py:95
  1.3 4.2 %collective-permute-start.1 = (bf16[32,4096]{1,0:T(8,128)(2,1)S(1)}, bf16[32,4096]{1,0:T(8,128)(2,1)S(1)}, u32[]{:S(2)}, u32[]{:S(2)}) collective-permute-start(bf16[32,4096]{1,0:T(8,128)(2,1)S(1)} %fusion.own_size), channel_id=1, source_target_pairs={{8,16},{24,32},{40,48},{56,64},{72,80},{88,96},{104,112},{120,128}... | collective-permute-start | bytes 786440 | tf_op jit(solution)/shard_map/ppermute | solution.py:213
  5.5 0.7 copy-done.6
  6.2 0.1 reshape.30
  6.3 0.1 constant_dynamic-slice_fusion
  6.3 0.2 copy.10
  6.5 0.1 reshape.31
  6.6 0.0 copy-start.4
  6.6 2.9 %collective-permute-done.1.near = bf16[32,4096]{1,0:T(8,128)(2,1)S(1)} collective-permute-done((bf16[32,4096]{1,0:T(8,128)(2,1)S(1)}, bf16[32,4096]{1,0:T(8,128)(2,1)S(1)}, u32[]{:S(2)}, u32[]{:S(2)}) %collective-permute-start.1) | collective-permute-done | bytes 262176 | tf_op jit(solution)/shard_map/ppermute | solution.py:213
  9.5 0.1 collective-permute-start.2
  9.6 0.2 fusion.1.twin_size
  9.9 0.0 copy-start.5
  9.9 1.4 %own_cross.1 = bf16[16,64,512]{2,1,0:T(8,128)(2,1)S(1)} custom-call(s32[129]{0:T(256)S(1)} %pad_add_fusion.blocks, bf16[2,32,96]{2,1,0:T(8,128)(2,1)S(1)} %copy-done.4, bf16[2,32,4096]{2,1,0:T(8,128)(2,1)S(1)} %bitcast.12, bf16[32,4096]{1,0:T(8,128)(2,1)S(1)} %collective-permute-done.1.near, bf16[32,4096]{1,0:T(8,128)(2,1)S(1)} %fusion.own_size, ...), custom_call_target="tpu_custom_call" | custom-call | tf_op jit(solution)/shard_map/own_cross/pallas_call | solution.py:224
  11.3 1.9 %twin_cross.1 = bf16[16,56,512]{2,1,0:T(8,128)(2,1)S(1)} custom-call(s32[129]{0:T(256)S(1)} %pad_add_fusion.blocks, bf16[2,32,96]{2,1,0:T(8,128)(2,1)S(1)} %copy-done.4, bf16[2,56,256]{2,1,0:T(8,128)(2,1)S(1)} %copy-done.5, bf16[2,32,4096]{2,1,0:T(8,128)(2,1)S(1)} %collective-permute-done.twin, bf16[32,4096]{1,0:T(8,128)(2,1)S(1)} %fusion.own_size, ...), custom_call_target="tpu_custom_call" | custom-call | tf_op jit(solution)/shard_map/twin_cross/pallas_call | solution.py:233
  13.3 0.0 copy-start.1
  13.3 23.1 %all_to_all.10.packed = bf16[16,56,512]{2,1,0:T(8,128)(2,1)S(1)} all-to-all(bf16[16,56,512]{2,1,0:T(8,128)(2,1)S(1)} %twin_cross.1), channel_id=1, replica_groups={{0,16,32,48,64,80,96,112,128,144,160,176,192,208,224,240},{8,24,40,56,7..., dimensions={0} | all-to-all | bytes 1835008 | tf_op jit(solution)/shard_map/all_to_all | solution.py:243
  36.4 2.1 %combine.1 = bf16[8,96,512]{2,1,0:T(8,128)(2,1)} custom-call(bf16[384,448]{1,0:T(8,128)(2,1)S(1)} %copy-done.1, bf16[384,448]{1,0:T(8,128)(2,1)S(1)} %copy-done.2, bf16[16,56,512]{2,1,0:T(8,128)(2,1)S(1)} %all_to_all.10.packed), custom_call_target="tpu_custom_call" | custom-call | tf_op jit(solution)/shard_map/combine/pallas_call | solution.py:244
  38.5 8.6 %all-to-all-start.1 = ((bf16[8,96,512]{2,1,0:T(8,128)(2,1)}), bf16[8,96,512]{2,1,0:T(8,128)(2,1)S(1)}, u32[]{:S(2)}, u32[]{:S(2)}) async-start(bf16[8,96,512]{2,1,0:T(8,128)(2,1)} %combine.1), calls=%async_computation.1 | async-start | bytes 1572864 | tf_op jit(solution)/shard_map/all_to_all | solution.py:256
  47.1 0.7 copy-done.7
  47.7 0.6 dynamic_slice.8
  48.3 0.6 compare_convert_fusion
  49.0 19.8 %all-to-all-done.1.parts = bf16[8,96,512]{2,1,0:T(8,128)(2,1)S(1)} async-done(((bf16[8,96,512]{2,1,0:T(8,128)(2,1)}), bf16[8,96,512]{2,1,0:T(8,128)(2,1)S(1)}, u32[]{:S(2)}, u32[]{:S(2)}) %all-to-all-start.1) | async-done | bytes 786464 | tf_op jit(solution)/shard_map/all_to_all | solution.py:256
  68.7 0.1 iota.7.live
  68.8 2.5 %stack.1 = f32[4,128,256]{2,1,0:T(8,128)} custom-call(f32[4,1,256]{2,1,0:T(1,128)S(1)} %iota.7.live, bf16[256,512]{1,0:T(8,128)(2,1)S(1)} %copy-done.3, bf16[8,96,512]{2,1,0:T(8,128)(2,1)S(1)} %all-to-all-done.1.parts), custom_call_target="tpu_custom_call" | custom-call | tf_op jit(solution)/shard_map/stack/pallas_call | solution.py:259
  (15 shorter events, 0.0 us)
Async XLA Ops:
  0.0 9.6 %collective-permute-start = (bf16[2,32,4096]{2,1,0:T(8,128)(2,1)}, bf16[2,32,4096]{2,1,0:T(8,128)(2,1)S(1)}, u32[]{:S(2)}, u32[]{:S(2)}) collective-permute-start(bf16[2,32,4096]{2,1,0:T(8,128)(2,1)} %bitcast.11), channel_id=1, source_target_pairs={{0,8},{8,0},{16,24},{24,16},{32,40},{40,32},{48,56},{56,48},{64,72... | collective-permute-start | bytes 1572872 | tf_op jit(solution)/shard_map/ppermute | solution.py:209
  1.3 8.3 %collective-permute-start.1 = (bf16[32,4096]{1,0:T(8,128)(2,1)S(1)}, bf16[32,4096]{1,0:T(8,128)(2,1)S(1)}, u32[]{:S(2)}, u32[]{:S(2)}) collective-permute-start(bf16[32,4096]{1,0:T(8,128)(2,1)S(1)} %fusion.own_size), channel_id=1, source_target_pairs={{8,16},{24,32},{40,48},{56,64},{72,80},{88,96},{104,112},{120,128}... | collective-permute-start | bytes 786440 | tf_op jit(solution)/shard_map/ppermute | solution.py:213
  5.5 0.7 copy-start.6
  6.2 3.7 %copy-start = (bf16[2,1,32,4096]{3,2,1,0:T(8,128)(2,1)S(1)}, bf16[2,1,32,4096]{3,2,1,0:T(8,128)(2,1)}, u32[]{:S(2)}) copy-start(bf16[2,1,32,4096]{3,2,1,0:T(8,128)(2,1)} %param.8) | copy-start | bytes 1572868
  6.6 3.2 %copy-start.4 = (bf16[2,32,96]{2,1,0:T(8,128)(2,1)S(1)}, bf16[2,32,96]{2,1,0:T(8,128)(2,1)}, u32[]{:S(2)}) copy-start(bf16[2,32,96]{2,1,0:T(8,128)(2,1)} %constant.38.clone.window) | copy-start | bytes 36868
  9.5 1.8 %collective-permute-start.2 = (bf16[32,4096]{1,0:T(8,128)(2,1)S(1)}, bf16[32,4096]{1,0:T(8,128)(2,1)S(1)}, u32[]{:S(2)}, u32[]{:S(2)}) collective-permute-start(bf16[32,4096]{1,0:T(8,128)(2,1)S(1)} %collective-permute-done.1.near), channel_id=1, source_target_pairs={{0,8},{8,0},{16,24},{24,16},{32,40},{40,32},{48,56},{56,48},{64,72... | collective-permute-start | bytes 786440 | tf_op jit(solution)/shard_map/ppermute | solution.py:214
  9.9 1.5 %copy-start.5 = (bf16[2,56,256]{2,1,0:T(8,128)(2,1)S(1)}, bf16[2,56,256]{2,1,0:T(8,128)(2,1)}, u32[]{:S(2)}) copy-start(bf16[2,56,256]{2,1,0:T(8,128)(2,1)} %constant.39.clone.compress) | copy-start | bytes 172036
  13.3 23.1 %copy-start.1 = (bf16[384,448]{1,0:T(8,128)(2,1)S(1)}, bf16[384,448]{1,0:T(8,128)(2,1)}, u32[]{:S(2)}) copy-start(bf16[384,448]{1,0:T(8,128)(2,1)} %constant.40.clone.high) | copy-start | bytes 1032196
  13.3 23.1 %copy-start.2 = (bf16[384,448]{1,0:T(8,128)(2,1)S(1)}, bf16[384,448]{1,0:T(8,128)(2,1)}, u32[]{:S(2)}) copy-start(bf16[384,448]{1,0:T(8,128)(2,1)} %constant.41.clone.low) | copy-start | bytes 1032196
  38.4 30.4 %copy-start.3 = (bf16[256,512]{1,0:T(8,128)(2,1)S(1)}, bf16[256,512]{1,0:T(8,128)(2,1)}, u32[]{:S(2)}) copy-start(bf16[256,512]{1,0:T(8,128)(2,1)} %constant.42.clone.expand) | copy-start | bytes 786436
  38.5 30.3 %all-to-all-start.1 = ((bf16[8,96,512]{2,1,0:T(8,128)(2,1)}), bf16[8,96,512]{2,1,0:T(8,128)(2,1)S(1)}, u32[]{:S(2)}, u32[]{:S(2)}) async-start(bf16[8,96,512]{2,1,0:T(8,128)(2,1)} %combine.1), calls=%async_computation.1 | async-start | bytes 1572864 | tf_op jit(solution)/shard_map/all_to_all | solution.py:256
  47.1 0.7 copy-start.7
